TPU v7x, 128 devices: a whole 4x4x4 slice. The times are simulated.
128 devices in a mesh: frame: 16 (over y_lo, z, core), row: 8 (over y_hi, x).
Axes of the slice: x: 4, y: 4 (y_hi: 2, y_lo: 2; y = y_hi * 2 + y_lo), z: 4, core: 2. Of those that a mesh axis runs over, the one named last changes fastest.
Arguments:
- video: bfloat16 [32, 16, 128, 384], P('frame', 'row'), may hold values from -30 to 30
- down_weight: bfloat16 [1152, 384], replicated, may hold values from -0.1875 to 0.1875
- conv_weight: bfloat16 [10368, 384], P(('frame', 'row')), may hold values from -0.0625 to 0.0625
- norm_gain_vector: float32 [384], replicated, may hold values from 0.1 to 1.9
- norm_shift_vector: float32 [384], replicated, may hold values from -3 to 3
- output_gradient: bfloat16 [16, 16, 128, 384], P(None, 'row', 'frame'), may hold values from -6 to 6
Outputs:
- encoded_code: bfloat16 [16, 16, 128, 384], P(None, 'row', 'frame')
- grad_video: bfloat16 [32, 16, 128, 384], P('frame', 'row')
- grad_conv: float32 [10368, 384], P(('frame', 'row'))
- grad_down: float32 [1152, 384], P(('frame', 'row'))
- gain_gradient: float32 [384], replicated
- grad_shift: float32 [384], replicated
All inputs are finite; a program needn't handle non-finite values.
Results may differ from a plain program's by a relative error of at most 0.004.
The roundings to bfloat16 on the way count: a program that leaves them out, or rounds other values in their place, can miss the bound.
Values may be sent and summed in bfloat16 or wider, within the bound.
A program may use at most 128 MiB of HBM per device.

v0:
```python
import jax
import jax.numpy as jnp
from jax import lax
from jax.sharding import PartitionSpec as P

CLUSTER_TALLY = 32


def from_behind(value, axis, steps):
    count = lax.axis_size(axis)
    first, last = (max(0, -steps), min(count, count - steps))
    return lax.ppermute(value, axis, [(source, source + steps) for source in range(first, last)])


def extended(block, sides, width):
    for axis, dim in sides:
        count = lax.axis_size(axis)
        forward = [(i, i + 1) for i in range(count - 1)]
        backward = [(target, source) for source, target in forward]
        low = lax.ppermute(
            lax.slice_in_dim(block, block.shape[dim] - width, None, axis=dim), axis, forward
        )
        high = lax.ppermute(lax.slice_in_dim(block, 0, width, axis=dim), axis, backward)
        block = jnp.concatenate([low, block, high], axis=dim)
    return block


def swish_derivative(before_nonlinearity):
    sigma = jax.nn.sigmoid(before_nonlinearity)
    return sigma * (1.0 + before_nonlinearity * (1.0 - sigma))


def contract_rows(left, right):
    return lax.dot_general(
        left, right, (((0,), (0,)), ((), ())), preferred_element_type=jnp.float32
    )


def contract_cols(left, right):
    return lax.dot_general(
        left, right, (((1,), (1,)), ((), ())), preferred_element_type=jnp.float32
    )


def forward_taps(padded, frames, height, width):
    pieces = []
    for a in range(3):
        for b in range(3):
            for e in range(3):
                pieces.append(padded[a : a + frames, b : b + height, e : e + width])
    joined = jnp.concatenate(pieces, -1)
    return joined.reshape(-1, joined.shape[-1])


def backward_taps(padded, frames, height, width):
    pieces = []
    for a in range(3):
        for b in range(3):
            for e in range(3):
                pieces.append(
                    padded[2 - a : 2 - a + frames, 2 - b : 2 - b + height, 2 - e : 2 - e + width]
                )
    joined = jnp.concatenate(pieces, -1)
    return joined.reshape(-1, joined.shape[-1])


def body(video, down_weight, conv_weight, norm_gain_vector, norm_shift_vector, output_gradient):
    chans = video.shape[3]
    cluster_width = chans // CLUSTER_TALLY
    frame_count = lax.axis_size("frame")
    row_count = lax.axis_size("row")
    devices = frame_count * row_count
    kernel_full = lax.all_gather(conv_weight, ("frame", "row"), axis=0, tiled=True)
    before = from_behind(video[1:2], "frame", 1)
    stacked = jnp.concatenate([before[0], video[0], video[1]], -1)
    slab_rows, slab_cols = (stacked.shape[0], stacked.shape[1])
    flat_in = stacked.reshape(-1, 3 * chans)
    down_frame = jnp.dot(flat_in, down_weight, preferred_element_type=jnp.float32)
    down_frame = down_frame.astype(jnp.bfloat16).reshape(1, slab_rows, slab_cols, chans)
    halved_clip = lax.all_to_all(down_frame, "frame", split_axis=2, concat_axis=0, tiled=True)
    halve_frames_routine = halved_clip.astype(jnp.float32)
    frames, height, width = (halved_clip.shape[0], halved_clip.shape[1], halved_clip.shape[2])
    total_sum, total_square = lax.psum(
        (
            jnp.sum(halve_frames_routine, (0, 1, 2)),
            jnp.sum(halve_frames_routine * halve_frames_routine, (0, 1, 2)),
        ),
        ("frame", "row"),
    )
    element_tally = frames * height * width * devices * cluster_width
    cluster_average = total_sum.reshape(CLUSTER_TALLY, cluster_width).sum(1) / element_tally
    cluster_squares = total_square.reshape(CLUSTER_TALLY, cluster_width).sum(1) / element_tally
    rstd_group = lax.rsqrt(cluster_squares - cluster_average * cluster_average + 1e-06)
    feature_average = jnp.repeat(cluster_average, cluster_width)
    feature_reciprocal_spread = jnp.repeat(rstd_group, cluster_width)
    standardized_source = (halve_frames_routine - feature_average) * feature_reciprocal_spread
    before_nonlinearity = standardized_source * norm_gain_vector + norm_shift_vector
    act = jax.nn.silu(before_nonlinearity).astype(jnp.bfloat16)
    bordered = extended(act, (("frame", 2), ("row", 1)), 1)
    padded = jnp.pad(bordered, ((2, 0), (0, 0), (0, 0), (0, 0)))
    tap_rows = forward_taps(padded, frames, height, width)
    residual_path = jnp.dot(tap_rows, kernel_full, preferred_element_type=jnp.float32).reshape(
        halve_frames_routine.shape
    )
    encoded_local = (halve_frames_routine + residual_path).astype(jnp.bfloat16)
    grad_flat = output_gradient.reshape(-1, chans)
    piece = tap_rows
    grad_conv = lax.psum_scatter(
        contract_rows(piece, grad_flat), ("frame", "row"), scatter_dimension=0, tiled=True
    )
    grad_border = extended(output_gradient, (("frame", 2), ("row", 1)), 1)
    grad_padded = jnp.pad(grad_border, ((0, 2), (0, 0), (0, 0), (0, 0)))
    flipped = kernel_full.reshape(27, chans, chans).transpose(0, 2, 1).reshape(27 * chans, chans)
    activation_cotangent = jnp.dot(
        backward_taps(grad_padded, frames, height, width),
        flipped,
        preferred_element_type=jnp.float32,
    )
    before_nonlinearity_cotangent = activation_cotangent.reshape(
        halve_frames_routine.shape
    ) * swish_derivative(before_nonlinearity)
    grad_shift, gain_gradient = lax.psum(
        (
            jnp.sum(before_nonlinearity_cotangent, (0, 1, 2)),
            jnp.sum(before_nonlinearity_cotangent * standardized_source, (0, 1, 2)),
        ),
        ("frame", "row"),
    )
    first_moment_mean = jnp.repeat(
        (norm_gain_vector * grad_shift).reshape(CLUSTER_TALLY, cluster_width).sum(1)
        / element_tally,
        cluster_width,
    )
    second_moment_mean = jnp.repeat(
        (norm_gain_vector * gain_gradient).reshape(CLUSTER_TALLY, cluster_width).sum(1)
        / element_tally,
        cluster_width,
    )
    latent_gradient = (
        output_gradient.astype(jnp.float32)
        + feature_reciprocal_spread
        * (
            before_nonlinearity_cotangent * norm_gain_vector
            - first_moment_mean
            - standardized_source * second_moment_mean
        )
    ).astype(jnp.bfloat16)
    latent_grad = lax.all_to_all(latent_gradient, "frame", split_axis=0, concat_axis=2, tiled=True)
    next_grad = from_behind(latent_grad, "frame", -1)
    latent_flat = latent_grad.reshape(-1, chans)
    next_flat = next_grad.reshape(-1, chans)
    even_grad = contract_cols(latent_flat, down_weight[chans : 2 * chans])
    odd_grad = contract_cols(latent_flat, down_weight[2 * chans :]) + contract_cols(
        next_flat, down_weight[:chans]
    )
    grad_video = jnp.stack([even_grad, odd_grad], 0).astype(jnp.bfloat16).reshape(video.shape)
    piece = flat_in
    grad_down = lax.psum_scatter(
        contract_rows(piece, latent_flat), ("frame", "row"), scatter_dimension=0, tiled=True
    )
    return (encoded_local, grad_video, grad_conv, grad_down, gain_gradient, grad_shift)


def solution(mesh):
    return jax.shard_map(
        body,
        mesh=mesh,
        in_specs=(
            P("frame", "row", None, None),
            P(),
            P(("frame", "row"), None),
            P(),
            P(),
            P(None, "row", "frame", None),
        ),
        out_specs=(
            P(None, "row", "frame", None),
            P("frame", "row", None, None),
            P(("frame", "row"), None),
            P(("frame", "row"), None),
            P(),
            P(),
        ),
        check_vma=False,
    )
```

profile of v0, /device:TPU:0, one launch (start us, length us, event | category | flops | bytes accessed | tf_op | source)
XLA Modules:
  0.0 1061.6 jit_solution(18363856912452407552)
XLA Ops:
  9.0 1.3 collective-permute-start.6
  10.3 3.0 collective-permute-start.5
  15.4 1.3 collective-permute-start.8
  16.7 4.6 collective-permute-start.7
  22.3 3.3 collective-permute-start
  26.5 1.6 maximum_maximum_fusion.1
  31.2 2.4 copy-done.19
  34.9 10.9 %all-to-all-start = ((bf16[1,2,128,384]{3,1,0,2:T(2,128)(2,1)}), bf16[1,2,128,384]{3,1,0,2:T(2,128)(2,1)S(1)}, u32[]{:S(2)}, u32[]{:S(2)}) async-start(bf16[1,2,128,384]{3,1,0,2:T(2,128)(2,1)} %copy.22), calls=%async_computation | async-start | bytes 393216 | tf_op jit(solution)/shard_map/all_to_all | solution.py:80
  46.6 6.6 all-to-all-done
  53.5 69.3 %all-reduce.6 = (f32[32,12]{1,0:T(8,128)S(1)}, f32[32,12]{1,0:T(8,128)S(1)}) all-reduce(f32[32,12]{1,0:T(8,128)S(1)} %reshape.80, f32[32,12]{1,0:T(8,128)S(1)} %reshape.79), channel_id=1, replica_groups=mesh['frame'=16,'row'=8] {'frame','row'}, use_global_device_ids=true, to_apply=%region_4.0 | all-reduce | flops 768 | bytes 6144 | tf_op jit(solution)/shard_map/psum | solution.py:83
  123.4 201.6 %all-gather.3.cloned.1.call-done = bf16[128,81,384]{2,1,0:T(8,128)(2,1)} async-done(((bf16[1,81,384]{2,1,0:T(8,128)(2,1)}), bf16[128,81,384]{2,1,0:T(8,128)(2,1)}) %all-gather.3.cloned.1.call-update) | async-done | bytes 7962640 | tf_op jit(solution)/shard_map/all_gather | solution.py:73
  325.0 9.7 reshape.81
  334.8 11.5 %copy.25 = bf16[27,384,384]{2,1,0:T(8,128)(2,1)} copy(bf16[27,384,384]{1,2,0:T(8,128)(2,1)} %bitcast.76) | data formatting | bytes 15925248 | tf_op jit(solution)/shard_map/transpose | solution.py:113
  346.3 7.2 fusion.45
  353.5 67.8 %all-reduce.5 = (f32[384]{0:T(512)S(1)}, f32[384]{0:T(512)S(1)}) all-reduce(f32[384]{0:T(512)S(1)} %get-tuple-element.7, f32[384]{0:T(512)S(1)} %get-tuple-element.6), channel_id=1, replica_groups=mesh['frame'=16,'row'=8] {'frame','row'}, use_global_device_ids=true, to_apply=%region_10.11 | all-reduce | flops 768 | bytes 6144 | tf_op jit(solution)/shard_map/psum | solution.py:122
  424.4 3.0 collective-permute-start.1
  429.9 4.6 collective-permute-start.3
  434.5 8.3 all-to-all-start.1
  443.0 9.7 reshape.91
  455.4 2.3 copy-done.20
  457.7 7.1 convolution_bitcast_fusion
  464.8 389.1 %fusion = f32[96,384]{1,0:T(8,128)S(1)} fusion(f32[10368,384]{1,0:T(8,128)} %convolution_bitcast_fusion), kind=kCustom, calls=%all-reduce-scatter | all-reduce-scatter fusion | flops 4718593 | bytes 16072704
  853.9 1.3 collective-permute-start.28
  855.3 1.3 collective-permute-start.27
  856.6 1.3 collective-permute-start.26
  857.9 1.3 collective-permute-start.25
  859.2 1.9 collective-permute-start.29
  864.3 1.3 collective-permute-start.23
  865.7 2.0 collective-permute-start.22
  867.6 20.6 %collective-permute-start.21 = (f32[96,384]{1,0:T(8,128)S(1)}, f32[96,384]{1,0:T(8,128)}, u32[]{:S(2)}, u32[]{:S(2)}) collective-permute-start(f32[96,384]{1,0:T(8,128)S(1)} %fusion), channel_id=1, source_target_pairs={{0,12},{1,13},{2,14},{3,15},{4,16},{5,17},{6,18},{7,19},{8,20},{9,... | collective-permute-start | bytes 442376
  888.3 2.0 collective-permute-start.20
  890.2 1.7 fusion.36
  892.0 6.7 collective-permute-start.19
  898.7 1.3 collective-permute-start.18
  900.0 2.0 collective-permute-start.17
  902.0 9.1 collective-permute-start.16
  911.1 1.3 collective-permute-start.15
  912.4 8.6 fusion.17
  921.1 3.8 collective-permute-start.14
  924.9 1.9 collective-permute-start.13
  926.8 4.2 collective-permute-start.12
  931.1 4.4 collective-permute-start.11
  935.5 2.0 collective-permute-start.10
  942.1 20.4 %concatenate.80 = f32[2001,384]{1,0:T(8,128)S(1)} concatenate(f32[81,384]{1,0:T(8,128)} %collective-permute-done.29, f32[96,384]{1,0:T(8,128)} %copy-done.3, f32[96,384]{1,0:T(8,128)} %copy-done.4, f32[96,384]{1,0:T(8,128)} %copy-done.5, f32[96,384]{1,0:T(8,128)} %copy-done.6, f32[96,384]{1,0:T(8,128)} %copy-done.7, f32[96,384]{1,0:T(8,128)} %copy-done.8, ...), dimensions={0} | concatenate | bytes 6147072
  963.9 1.5 fusion.16
  965.4 1.7 pad_maximum_fusion.5
  967.1 86.3 %all-reduce.9.cloned.1.call-done = f32[1152,384]{1,0:T(8,128)} async-done(((f32[1152,384]{1,0:T(8,128)}), f32[1152,384]{1,0:T(8,128)}) %all-reduce.9.cloned.1.call-update) | async-done | bytes 1769488
  1053.4 1.4 constant_dynamic-slice_fusion.1
  (179 shorter events, 29.4 us)
Async XLA Ops:
  7.2 317.9 %all-gather.3.cloned.1.call-start = ((), (), s32[]{:S(2)}) async-start(), calls=%async_computation.2 | async-start | bytes 8718336 | tf_op jit(solution)/shard_map/all_gather | solution.py:73
  9.0 4.3 collective-permute-start.6
  10.3 3.9 collective-permute-start.5
  15.4 10.2 collective-permute-start.8
  16.7 9.8 collective-permute-start.7
  22.3 8.8 collective-permute-start
  34.9 18.3 %all-to-all-start = ((bf16[1,2,128,384]{3,1,0,2:T(2,128)(2,1)}), bf16[1,2,128,384]{3,1,0,2:T(2,128)(2,1)S(1)}, u32[]{:S(2)}, u32[]{:S(2)}) async-start(bf16[1,2,128,384]{3,1,0,2:T(2,128)(2,1)} %copy.22), calls=%async_computation | async-start | bytes 393216 | tf_op jit(solution)/shard_map/all_to_all | solution.py:80
  334.7 11.5 %copy-start.18 = (f32[384]{0:T(512)S(1)}, f32[384]{0:T(512)}, u32[]{:S(2)}) copy-start(f32[384]{0:T(512)} %param.9) | copy-start | bytes 4612
  334.8 11.5 %copy-start.21 = (f32[384]{0:T(512)S(1)}, f32[384]{0:T(512)}, u32[]{:S(2)}) copy-start(f32[384]{0:T(512)} %param.10) | copy-start | bytes 4612
  421.3 31.5 %copy-start.22 = (f32[384]{0:T(512)}, f32[384]{0:T(512)S(1)}, u32[]{:S(2)}) copy-start(f32[384]{0:T(512)S(1)} %get-tuple-element.8) | copy-start | bytes 4612
  421.3 31.5 %copy-start.23 = (f32[384]{0:T(512)}, f32[384]{0:T(512)S(1)}, u32[]{:S(2)}) copy-start(f32[384]{0:T(512)S(1)} %get-tuple-element.9) | copy-start | bytes 4612
  423.1 4.3 collective-permute-start.2
  424.4 3.9 collective-permute-start.1
  428.6 24.2 %collective-permute-start.4 = (bf16[16,1,10,384]{3,2,1,0:T(8,128)(2,1)S(1)}, bf16[16,1,10,384]{3,2,1,0:T(8,128)(2,1)S(1)}, u32[]{:S(2)}, u32[]{:S(2)}) collective-permute-start(bf16[16,1,10,384]{3,2,1,0:T(8,128)(2,1)S(1)} %get-tuple-element.17), channel_id=1, source_target_pairs={{1,0},{2,1},{3,2},{4,3},{5,4},{6,5},{7,6},{9,8},{10,9},{11,10},{12... | collective-permute-start | bytes 368648 | tf_op jit(solution)/shard_map/ppermute | solution.py:23
  429.9 22.9 %collective-permute-start.3 = (bf16[16,1,10,384]{3,2,1,0:T(8,128)(2,1)S(1)}, bf16[16,1,10,384]{3,2,1,0:T(8,128)(2,1)S(1)}, u32[]{:S(2)}, u32[]{:S(2)}) collective-permute-start(bf16[16,1,10,384]{3,2,1,0:T(8,128)(2,1)S(1)} %get-tuple-element.16), channel_id=1, source_target_pairs={{0,1},{1,2},{2,3},{3,4},{4,5},{5,6},{6,7},{8,9},{9,10},{10,11},{11... | collective-permute-start | bytes 368648 | tf_op jit(solution)/shard_map/ppermute | solution.py:20
  434.5 426.7 %all-to-all-start.1 = ((bf16[16,2,8,384]{3,2,1,0:T(8,128)(2,1)}), bf16[16,2,8,384]{3,2,1,0:T(8,128)(2,1)S(1)}, u32[]{:S(2)}, u32[]{:S(2)}) async-start(bf16[16,2,8,384]{3,2,1,0:T(8,128)(2,1)} %get-tuple-element.12), calls=%async_computation.1 | async-start | bytes 393216 | tf_op jit(solution)/shard_map/all_to_all | solution.py:148
  442.8 610.6 %all-reduce.9.cloned.1.call-start = ((), (), s32[]{:S(2)}) async-start(), calls=%async_computation.3 | async-start | bytes 3538944
  853.9 10.4 collective-permute-start.28
  855.3 10.4 collective-permute-start.27
  856.6 11.1 %collective-permute-start.26 = (f32[96,384]{1,0:T(8,128)S(1)}, f32[96,384]{1,0:T(8,128)S(1)}, u32[]{:S(2)}, u32[]{:S(2)}) collective-permute-start(f32[96,384]{1,0:T(8,128)S(1)} %fusion), channel_id=1, source_target_pairs={{0,17},{1,18},{2,19},{3,20},{4,21},{5,22},{6,23},{7,24},{8,25},{9,... | collective-permute-start | bytes 442376
  857.9 30.4 %collective-permute-start.25 = (f32[96,384]{1,0:T(8,128)S(1)}, f32[96,384]{1,0:T(8,128)S(1)}, u32[]{:S(2)}, u32[]{:S(2)}) collective-permute-start(f32[96,384]{1,0:T(8,128)S(1)} %fusion), channel_id=1, source_target_pairs={{0,16},{1,17},{2,18},{3,19},{4,20},{5,21},{6,22},{7,23},{8,24},{9,... | collective-permute-start | bytes 442376
  859.2 3.8 collective-permute-start.29
  863.0 29.0 %collective-permute-start.24 = (f32[96,384]{1,0:T(8,128)S(1)}, f32[96,384]{1,0:T(8,128)S(1)}, u32[]{:S(2)}, u32[]{:S(2)}) collective-permute-start(f32[96,384]{1,0:T(8,128)S(1)} %fusion), channel_id=1, source_target_pairs={{0,15},{1,16},{2,17},{3,18},{4,19},{5,20},{6,21},{7,22},{8,23},{9,... | collective-permute-start | bytes 442376
  864.3 56.7 %copy-start.3 = (f32[96,384]{1,0:T(8,128)}, f32[96,384]{1,0:T(8,128)S(1)}, u32[]{:S(2)}) copy-start(f32[96,384]{1,0:T(8,128)S(1)} %collective-permute-done.28) | copy-start | bytes 442372
  864.3 34.4 %collective-permute-start.23 = (f32[96,384]{1,0:T(8,128)S(1)}, f32[96,384]{1,0:T(8,128)S(1)}, u32[]{:S(2)}, u32[]{:S(2)}) collective-permute-start(f32[96,384]{1,0:T(8,128)S(1)} %fusion), channel_id=1, source_target_pairs={{0,14},{1,15},{2,16},{3,17},{4,18},{5,19},{6,20},{7,21},{8,22},{9,... | collective-permute-start | bytes 442376
  865.6 55.4 %copy-start.4 = (f32[96,384]{1,0:T(8,128)}, f32[96,384]{1,0:T(8,128)S(1)}, u32[]{:S(2)}) copy-start(f32[96,384]{1,0:T(8,128)S(1)} %collective-permute-done.27) | copy-start | bytes 442372
  865.7 34.4 %collective-permute-start.22 = (f32[96,384]{1,0:T(8,128)S(1)}, f32[96,384]{1,0:T(8,128)}, u32[]{:S(2)}, u32[]{:S(2)}) collective-permute-start(f32[96,384]{1,0:T(8,128)S(1)} %fusion), channel_id=1, source_target_pairs={{0,13},{1,14},{2,15},{3,16},{4,17},{5,18},{6,19},{7,20},{8,21},{9,... | collective-permute-start | bytes 442376
  867.6 53.4 %copy-start.5 = (f32[96,384]{1,0:T(8,128)}, f32[96,384]{1,0:T(8,128)S(1)}, u32[]{:S(2)}) copy-start(f32[96,384]{1,0:T(8,128)S(1)} %collective-permute-done.26) | copy-start | bytes 442372
  867.6 34.4 %collective-permute-start.21 = (f32[96,384]{1,0:T(8,128)S(1)}, f32[96,384]{1,0:T(8,128)}, u32[]{:S(2)}, u32[]{:S(2)}) collective-permute-start(f32[96,384]{1,0:T(8,128)S(1)} %fusion), channel_id=1, source_target_pairs={{0,12},{1,13},{2,14},{3,15},{4,16},{5,17},{6,18},{7,19},{8,20},{9,... | collective-permute-start | bytes 442376
  888.3 32.7 %copy-start.6 = (f32[96,384]{1,0:T(8,128)}, f32[96,384]{1,0:T(8,128)S(1)}, u32[]{:S(2)}) copy-start(f32[96,384]{1,0:T(8,128)S(1)} %collective-permute-done.25) | copy-start | bytes 442372
  888.3 22.9 %collective-permute-start.20 = (f32[96,384]{1,0:T(8,128)S(1)}, f32[96,384]{1,0:T(8,128)}, u32[]{:S(2)}, u32[]{:S(2)}) collective-permute-start(f32[96,384]{1,0:T(8,128)S(1)} %fusion), channel_id=1, source_target_pairs={{0,11},{1,12},{2,13},{3,14},{4,15},{5,16},{6,17},{7,18},{8,19},{9,... | collective-permute-start | bytes 442376
  892.0 29.0 %copy-start.7 = (f32[96,384]{1,0:T(8,128)}, f32[96,384]{1,0:T(8,128)S(1)}, u32[]{:S(2)}) copy-start(f32[96,384]{1,0:T(8,128)S(1)} %collective-permute-done.24) | copy-start | bytes 442372
  892.0 29.1 %collective-permute-start.19 = (f32[96,384]{1,0:T(8,128)S(1)}, f32[96,384]{1,0:T(8,128)S(1)}, u32[]{:S(2)}, u32[]{:S(2)}) collective-permute-start(f32[96,384]{1,0:T(8,128)S(1)} %fusion), channel_id=1, source_target_pairs={{0,10},{1,11},{2,12},{3,13},{4,14},{5,15},{6,16},{7,17},{8,18},{9,... | collective-permute-start | bytes 442376
  898.7 22.3 %copy-start.8 = (f32[96,384]{1,0:T(8,128)}, f32[96,384]{1,0:T(8,128)S(1)}, u32[]{:S(2)}) copy-start(f32[96,384]{1,0:T(8,128)S(1)} %collective-permute-done.23) | copy-start | bytes 442372
  898.7 26.1 %collective-permute-start.18 = (f32[96,384]{1,0:T(8,128)S(1)}, f32[96,384]{1,0:T(8,128)S(1)}, u32[]{:S(2)}, u32[]{:S(2)}) collective-permute-start(f32[96,384]{1,0:T(8,128)S(1)} %fusion), channel_id=1, source_target_pairs={{0,9},{1,10},{2,11},{3,12},{4,13},{5,14},{6,15},{7,16},{8,17},{9,1... | collective-permute-start | bytes 442376
  900.0 26.8 %collective-permute-start.17 = (f32[96,384]{1,0:T(8,128)S(1)}, f32[96,384]{1,0:T(8,128)S(1)}, u32[]{:S(2)}, u32[]{:S(2)}) collective-permute-start(f32[96,384]{1,0:T(8,128)S(1)} %fusion), channel_id=1, source_target_pairs={{0,8},{1,9},{2,10},{3,11},{4,12},{5,13},{6,14},{7,15},{8,16},{9,17... | collective-permute-start | bytes 442376
  902.0 29.0 %collective-permute-start.16 = (f32[96,384]{1,0:T(8,128)S(1)}, f32[96,384]{1,0:T(8,128)S(1)}, u32[]{:S(2)}, u32[]{:S(2)}) collective-permute-start(f32[96,384]{1,0:T(8,128)S(1)} %fusion), channel_id=1, source_target_pairs={{0,7},{1,8},{2,9},{3,10},{4,11},{5,12},{6,13},{7,14},{8,15},{9,16}... | collective-permute-start | bytes 442376
  911.1 24.3 %collective-permute-start.15 = (f32[96,384]{1,0:T(8,128)S(1)}, f32[96,384]{1,0:T(8,128)S(1)}, u32[]{:S(2)}, u32[]{:S(2)}) collective-permute-start(f32[96,384]{1,0:T(8,128)S(1)} %fusion), channel_id=1, source_target_pairs={{0,6},{1,7},{2,8},{3,9},{4,10},{5,11},{6,12},{7,13},{8,14},{9,15},... | collective-permute-start | bytes 442376
  921.1 19.7 %copy-start.9 = (f32[96,384]{1,0:T(8,128)}, f32[96,384]{1,0:T(8,128)S(1)}, u32[]{:S(2)}) copy-start(f32[96,384]{1,0:T(8,128)S(1)} %collective-permute-done.19) | copy-start | bytes 442372
  921.1 17.4 %collective-permute-start.14 = (f32[96,384]{1,0:T(8,128)S(1)}, f32[96,384]{1,0:T(8,128)S(1)}, u32[]{:S(2)}, u32[]{:S(2)}) collective-permute-start(f32[96,384]{1,0:T(8,128)S(1)} %fusion), channel_id=1, source_target_pairs={{0,5},{1,6},{2,7},{3,8},{4,9},{5,10},{6,11},{7,12},{8,13},{9,14},{... | collective-permute-start | bytes 442376
  924.8 16.0 %copy-start.10 = (f32[96,384]{1,0:T(8,128)}, f32[96,384]{1,0:T(8,128)S(1)}, u32[]{:S(2)}) copy-start(f32[96,384]{1,0:T(8,128)S(1)} %collective-permute-done.18) | copy-start | bytes 442372
  924.9 15.9 %collective-permute-start.13 = (f32[96,384]{1,0:T(8,128)S(1)}, f32[96,384]{1,0:T(8,128)S(1)}, u32[]{:S(2)}, u32[]{:S(2)}) collective-permute-start(f32[96,384]{1,0:T(8,128)S(1)} %fusion), channel_id=1, source_target_pairs={{0,4},{1,5},{2,6},{3,7},{4,8},{5,9},{6,10},{7,11},{8,12},{9,13},{1... | collective-permute-start | bytes 442376
  926.8 14.0 %copy-start.11 = (f32[96,384]{1,0:T(8,128)}, f32[96,384]{1,0:T(8,128)S(1)}, u32[]{:S(2)}) copy-start(f32[96,384]{1,0:T(8,128)S(1)} %collective-permute-done.17) | copy-start | bytes 442372
  926.8 14.0 %collective-permute-start.12 = (f32[96,384]{1,0:T(8,128)S(1)}, f32[96,384]{1,0:T(8,128)S(1)}, u32[]{:S(2)}, u32[]{:S(2)}) collective-permute-start(f32[96,384]{1,0:T(8,128)S(1)} %fusion), channel_id=1, source_target_pairs={{0,3},{1,4},{2,5},{3,6},{4,7},{5,8},{6,9},{7,10},{8,11},{9,12},{10... | collective-permute-start | bytes 442376
  931.1 9.8 copy-start.12
  931.1 9.7 collective-permute-start.11
  935.5 6.6 collective-permute-start.10
  938.5 24.8 %collective-permute-start.9 = (bf16[1,2,128,384]{3,2,1,0:T(8,128)(2,1)}, bf16[1,2,128,384]{3,2,1,0:T(8,128)(2,1)S(1)}, u32[]{:S(2)}, u32[]{:S(2)}) collective-permute-start(bf16[1,2,128,384]{3,2,1,0:T(8,128)(2,1)} %get-tuple-element.24), channel_id=1, source_target_pairs={{8,0},{16,8},{24,16},{32,24},{40,32},{48,40},{56,48},{64,56},{72,6... | collective-permute-start | bytes 589832 | tf_op jit(solution)/shard_map/ppermute | solution.py:12
  (10 other events, 22.1 us)
Sparse Core Ops, SparseCore 0:
  9.7 315.2 all-gather.2
  892.1 161.2 all-reduce.8
where the time goes:
time: 1070 us; the launch traced here: 1060 us
  blocking collectives  526 us (49%)
  waiting for transfers between devices  299 us (28%)
  starting transfers between devices  115 us (11%)
  local copies, waits for them, and re-layouts  69 us (6%)
  matrix products  28.5 us (3%)
  between operations  15 us (1%)
    unnamed x1, blocking collectives  389 us
    all_gather x1, waiting for transfers between devices, body(): lax.all_gather(conv_weight, ('frame', 'row'), axis=0, tiled=True)  202 us
    unnamed x23, waiting for transfers between devices  88.3 us
    unnamed x21, starting transfers between devices  71.1 us
    psum x1, blocking collectives, body(): lax.psum((jnp.sum(halve_frames_routine, (0, 1, 2)), jnp.sum(halve_frames_...  69.3 us
    psum x1, blocking collectives, body(): lax.psum((jnp.sum(before_nonlinearity_cotangent, (0, 1, 2)), jnp.sum(befo...  67.8 us
    unnamed x101, local copies, waits for them, and re-layouts  41.9 us
  transfers between devices with their start and end apart: 34, of which 7 were waited for; matrix products, arithmetic and copies ran while one was open for 43% of the time, Pallas kernels for 0%

commit v1 on v0

--- a/solution.py
+++ b/solution.py
@@ -1,7 +1,389 @@
+import functools
 import jax
 import jax.numpy as jnp
 from jax import lax
+from jax.experimental import pallas as pl
+from jax.experimental.pallas import tpu as pltpu
 from jax.sharding import PartitionSpec as P
+
+MESH = pl.DeviceIdType.MESH
+AXES = "xyz"
+ORDERS = ("xyz", "yzx", "zxy")
+BLOCK = 96
+LANES = 128
+
+
+def position():
+    f, r = lax.axis_index("frame"), lax.axis_index("row")
+    y = lax.div(r, 4) * 2 + lax.div(f, 8)
+    pos = {"x": lax.rem(r, 4), "y": y, "z": lax.rem(lax.div(f, 2), 4)}
+    return f, r, pos, lax.rem(f, 2)
+
+
+def device_at(pos, core):
+    frame = lax.rem(pos["y"], 2) * 8 + pos["z"] * 2 + core
+    row = lax.div(pos["y"], 2) * 4 + pos["x"]
+    return (frame, row)
+
+
+def shifted(pos, axis, steps):
+    moved = dict(pos)
+    moved[axis] = lax.rem(pos[axis] + (steps + 4), 4)
+    return moved
+
+
+def chip_neighbours(pos, core):
+    near = [device_at(shifted(pos, axis, s), core) for axis in AXES for s in (1, -1)]
+    return near + [device_at(pos, 1 - core)]
+
+
+def greet(devices):
+    barrier = pltpu.get_barrier_semaphore()
+    for device in devices:
+        pl.semaphore_signal(barrier, inc=1, device_id=device, device_id_type=MESH)
+    pl.semaphore_wait(barrier, len(devices))
+
+
+def remote(src, dst, sems, index, device):
+    return pltpu.make_async_remote_copy(
+        src_ref=src,
+        dst_ref=dst,
+        send_sem=sems[0].at[index],
+        recv_sem=sems[1].at[index],
+        device_id=device,
+        device_id_type=MESH,
+    )
+
+
+GATHER_COPIES = 16
+
+
+def gather_steps(pos, core, order, buf, sems, base):
+    a, b, c = order
+    ca, cb, cc = pos[a], pos[b], pos[c]
+    sent = []
+
+    def start(src, dst, device):
+        op = remote(src, dst, sems, base + len(sent), device)
+        op.start()
+        sent.append(op)
+        return op
+
+    whole = {
+        c: lambda i: buf.at[core, ca, cb, i],
+        b: lambda i: buf.at[core, ca, i],
+        a: lambda i: buf.at[core, i],
+    }
+    half = BLOCK // 2
+    parts = {
+        c: lambda i, h: buf.at[core, ca, cb, i, pl.ds(h * half, half)],
+        b: lambda i, h: buf.at[core, ca, i, pl.ds(2 * h, 2)],
+        a: lambda i, h: buf.at[core, i, pl.ds(2 * h, 2)],
+    }
+    other = device_at(pos, 1 - core)
+    for axis in (c, b, a):
+        me = pos[axis]
+        up, down = shifted(pos, axis, 1), shifted(pos, axis, -1)
+        mine, one, ref = whole[axis](me), whole[axis], parts[axis]
+        first = start(mine, mine, device_at(up, core))
+        second = start(mine, mine, device_at(down, core))
+        if axis == a:
+            start(mine, mine, other)
+        yield
+        first.wait_recv()
+        third = start(ref(down[axis], 0), ref(down[axis], 0), device_at(up, core))
+        if axis == a:
+            start(one(down[axis]), one(down[axis]), other)
+        second.wait_recv()
+        fourth = start(ref(up[axis], 1), ref(up[axis], 1), device_at(down, core))
+        if axis == a:
+            start(one(up[axis]), one(up[axis]), other)
+        yield
+        third.wait_recv()
+        fourth.wait_recv()
+    far = shifted(pos, a, 2)[a]
+    start(buf.at[core, far], buf.at[core, far], other)
+    yield
+    for k, op in enumerate(sent):
+        if k in (10, 12, 14, 15):
+            op.wait_recv()
+        op.wait_send()
+
+
+def interleave(steps):
+    steps = list(steps)
+    while steps:
+        left = []
+        for step in steps:
+            try:
+                next(step)
+                left.append(step)
+            except StopIteration:
+                pass
+        steps = left
+
+
+def static_place(d, order):
+    x, y_hi, core = d % 4, (d // 4) % 2, (d // 8) % 2
+    return core, x, y_hi
+
+
+def gather_kernel(w_ref, out_ref, b0, b1, b2, wide, send, recv):
+    f, r, pos, core = position()
+    bufs = (b0, b1, b2)
+    greet(chip_neighbours(pos, core))
+    for j, order in enumerate(ORDERS):
+        a, b, c = order
+        bufs[j][core, pos[a], pos[b], pos[c]] = w_ref[j]
+    interleave(
+        gather_steps(pos, core, order, bufs[j], (send, recv), j * GATHER_COPIES)
+        for j, order in enumerate(ORDERS)
+    )
+
+    def unpack(g, _):
+        y_lo, z = lax.div(g, 4), lax.rem(g, 4)
+        for i in range(16):
+            at = {"x": i % 4, "y": 2 * ((i // 4) % 2) + y_lo, "z": z}
+            for j, (a, b, c) in enumerate(ORDERS):
+                block = bufs[j][i // 8, at[a], at[b], at[c]].astype(jnp.float32)
+                wide[81 * i : 81 * i + 81, LANES * j : LANES * (j + 1)] = block[:81]
+        out_ref[pl.ds(pl.multiple_of(g * 1296, 16), 1296)] = wide[...].astype(jnp.bfloat16)
+        return 0
+
+    lax.fori_loop(0, 8, unpack, 0)
+
+
+def gather_weights(w):
+    padded = jnp.pad(w, ((0, BLOCK - w.shape[0]), (0, 0)))
+    split = padded.reshape(BLOCK, 3, LANES).transpose(1, 0, 2)
+    buf = pltpu.VMEM((2, 4, 4, 4, BLOCK, LANES), jnp.bfloat16)
+    return pl.pallas_call(
+        gather_kernel,
+        out_shape=jax.ShapeDtypeStruct((10368, 384), jnp.bfloat16),
+        in_specs=[pl.BlockSpec(memory_space=pltpu.VMEM)],
+        out_specs=pl.BlockSpec(memory_space=pltpu.VMEM),
+        scratch_shapes=[buf, buf, buf, pltpu.VMEM((1296, 384), jnp.float32),
+                        pltpu.SemaphoreType.DMA((3 * GATHER_COPIES,)),
+                        pltpu.SemaphoreType.DMA((3 * GATHER_COPIES,))],
+        compiler_params=pltpu.CompilerParams(
+            collective_id=0, has_side_effects=True, vmem_limit_bytes=60 * 2**20),
+    )(split)
+
+
+SCATTER_COPIES = 16
+
+
+def add_into(count, target, terms):
+    def step(i, _):
+        total = terms[0](i).astype(jnp.float32)
+        for term in terms[1:]:
+            total = total + term(i).astype(jnp.float32)
+        target(i, total)
+        return 0
+
+    lax.fori_loop(0, count, step, 0)
+
+
+def scatter_steps(pos, core, order, rows, piles, got, near, q, near_q, u, near_u, sems, base, out):
+    a, b, c = order
+    ca, cb, cc = pos[a], pos[b], pos[c]
+    half = rows // 2
+    sent = []
+
+    def start(src, dst, device):
+        op = remote(src, dst, sems, base + len(sent), device)
+        op.start()
+        sent.append(op)
+        return op
+
+    def toward(axis, steps):
+        return device_at(shifted(pos, axis, steps), core)
+
+    def at(axis, steps):
+        return shifted(pos, axis, steps)[axis]
+
+    other = device_at(pos, 1 - core)
+    far, up, down = at(a, 2), at(a, 1), at(a, -1)
+    swaps = [start(piles.at[1 - core, i], got.at[i], other) for i in (far, up, down, ca)]
+    yield
+
+    def store(i):
+        def put(k, total):
+            piles[core, i, k] = total.astype(jnp.bfloat16)
+        return put
+
+    def pair(i, first=0):
+        return [lambda k: piles[core, i, k + first], lambda k: got[i, k + first]]
+
+    near_a, near_b, near_c, near_d = near
+    swaps[0].wait_recv()
+    add_into(4, store(far), pair(far))
+    op_a = start(piles.at[core, far, pl.ds(0, 2)], near_a, toward(a, 1))
+    op_b = start(piles.at[core, far, pl.ds(2, 2)], near_b, toward(a, -1))
+    yield
+    swaps[1].wait_recv()
+    op_a.wait_recv()
+    add_into(2, store(up), pair(up) + [lambda k: near_a[k]])
+    add_into(2, lambda k, total: store(up)(k + 2, total), pair(up, 2))
+    op_c = start(piles.at[core, up], near_c, toward(a, 1))
+    swaps[2].wait_recv()
+    op_b.wait_recv()
+    add_into(2, store(down), pair(down))
+    add_into(2, lambda k, total: store(down)(k + 2, total), pair(down, 2) + [lambda k: near_b[k]])
+    op_d = start(piles.at[core, down], near_d, toward(a, -1))
+    yield
+    swaps[3].wait_recv()
+    op_c.wait_recv()
+    op_d.wait_recv()
+
+    def put_q(k, total):
+        q[k] = total
+
+    add_into(4, put_q, pair(ca) + [lambda k: near_c[k], lambda k: near_d[k]])
+    for axis, v, near_v, low, high, lower, upper in (
+        (b, q, near_q, lambda i: q.at[i, pl.ds(0, 2)], lambda i: q.at[i, pl.ds(2, 2)],
+         pl.ds(0, 2), pl.ds(2, 2)),
+        (c, u, near_u, lambda i: u.at[i, pl.ds(0, half)], lambda i: u.at[i, pl.ds(half, half)],
+         pl.ds(0, half), pl.ds(half, half)),
+    ):
+        far, up, down, me = at(axis, 2), at(axis, 1), at(axis, -1), pos[axis]
+        near_a, near_b, near_c, near_d = near_v
+        op_a = start(low(far), near_a, toward(axis, 1))
+        op_b = start(high(far), near_b, toward(axis, -1))
+        yield
+        op_a.wait_recv()
+        v[up, lower] = v[up, lower] + near_a[...]
+        op_c = start(v.at[up], near_c, toward(axis, 1))
+        op_b.wait_recv()
+        v[down, upper] = v[down, upper] + near_b[...]
+        op_d = start(v.at[down], near_d, toward(axis, -1))
+        yield
+        op_c.wait_recv()
+        op_d.wait_recv()
+        total = v[me] + near_c[...] + near_d[...]
+        if axis == b:
+            u[...] = total
+        else:
+            out(total)
+    yield
+    for op in sent:
+        op.wait_send()
+
+
+def scatter_scratch(rows):
+    def bf(*lead):
+        return pltpu.VMEM(lead + (rows, LANES), jnp.bfloat16)
+
+    def f32(*lead):
+        return pltpu.VMEM(lead + (rows, LANES), jnp.float32)
+
+    half = pltpu.VMEM((rows // 2, LANES), jnp.float32)
+    one = [bf(2, 4, 4, 4), bf(4, 4, 4), bf(2, 4), bf(2, 4), bf(4, 4), bf(4, 4), f32(4, 4),
+           f32(2), f32(2), f32(4), f32(4), f32(4), half, half, f32(), f32()]
+    return one
+
+
+def scatter_kernel(rows, gc_ref, gd_ref, out_ref, *scratch):
+    f, r, pos, core = position()
+    size = (len(scratch) - 2) // 3
+    sets = [scratch[j * size : (j + 1) * size] for j in range(3)]
+    send, recv = scratch[-2:]
+    greet(chip_neighbours(pos, core))
+
+    def pack(g, _):
+        y_lo, z = lax.div(g, 4), lax.rem(g, 4)
+        wide = gc_ref.at[pl.ds(pl.multiple_of(g * 1296, 16), 1296)]
+        thin = gd_ref.at[pl.ds(pl.multiple_of(g * 144, 16), 144)]
+        for i in range(16):
+            at = {"x": i % 4, "y": 2 * ((i // 4) % 2) + y_lo, "z": z}
+            for j, (a, b, c) in enumerate(ORDERS):
+                cols = slice(LANES * j, LANES * (j + 1))
+                block = jnp.concatenate(
+                    [wide[81 * i : 81 * i + 81, cols], thin[9 * i : 9 * i + 9, cols],
+                     jnp.zeros((6, LANES), jnp.float32)], 0)
+                sets[j][0][i // 8, at[a], at[b], at[c]] = block.astype(jnp.bfloat16)
+        return 0
+
+    lax.fori_loop(0, 8, pack, 0)
+
+    def run(j, order):
+        s = sets[j]
+
+        def out(total):
+            out_ref[:, LANES * j : LANES * (j + 1)] = total
+
+        return scatter_steps(pos, core, order, rows, s[0], s[1], s[2:6], s[6], s[7:11],
+                             s[11], s[12:16], (send, recv), j * SCATTER_COPIES, out)
+
+    interleave(run(j, order) for j, order in enumerate(ORDERS))
+
+
+def scatter_sum(gc, gd):
+    vmem = pl.BlockSpec(memory_space=pltpu.VMEM)
+    return pl.pallas_call(
+        functools.partial(scatter_kernel, BLOCK),
+        out_shape=jax.ShapeDtypeStruct((BLOCK, 384), jnp.float32),
+        in_specs=[vmem, vmem],
+        out_specs=vmem,
+        scratch_shapes=scatter_scratch(BLOCK) * 3 + [
+            pltpu.SemaphoreType.DMA((3 * SCATTER_COPIES,)),
+            pltpu.SemaphoreType.DMA((3 * SCATTER_COPIES,))],
+        compiler_params=pltpu.CompilerParams(
+            collective_id=1, has_side_effects=True, vmem_limit_bytes=60 * 2**20),
+    )(gc, gd)
+
+
+def sum_steps(f, r, x_ref, out_ref, row_in, frame_in, row_total, sems, base=0):
+    row_in[r] = x_ref[...]
+    ops = []
+    for s in range(1, 8):
+        peer = lax.rem(r + s, 8)
+        op = remote(row_in.at[r], row_in.at[r], sems, base + s - 1, (f, peer))
+        op.start()
+        ops.append(op)
+    yield
+    for op in ops:
+        op.wait_recv()
+    total = row_in[0]
+    for s in range(1, 8):
+        total = total + row_in[s]
+    frame_in[f] = total
+    more = []
+    for s in range(1, 16):
+        peer = lax.rem(f + s, 16)
+        op = remote(frame_in.at[f], frame_in.at[f], sems, base + 6 + s, (peer, r))
+        op.start()
+        more.append(op)
+    yield
+    for op in more:
+        op.wait_recv()
+    total = frame_in[0]
+    for s in range(1, 16):
+        total = total + frame_in[s]
+    out_ref[...] = total
+    for op in ops + more:
+        op.wait_send()
+
+
+def sum_kernel(x_ref, out_ref, row_in, frame_in, send, recv):
+    f, r = lax.axis_index("frame"), lax.axis_index("row")
+    greet([(f, lax.rem(r + s, 8)) for s in range(1, 8)]
+          + [(lax.rem(f + s, 16), r) for s in range(1, 16)])
+    interleave([sum_steps(f, r, x_ref, out_ref, row_in, frame_in, None, (send, recv))])
+
+
+def all_sum(x):
+    vmem = pl.BlockSpec(memory_space=pltpu.VMEM)
+    return pl.pallas_call(
+        sum_kernel,
+        out_shape=jax.ShapeDtypeStruct((8, 384), jnp.float32),
+        in_specs=[vmem],
+        out_specs=vmem,
+        scratch_shapes=[pltpu.VMEM((8, 8, 384), jnp.float32), pltpu.VMEM((16, 8, 384), jnp.float32),
+                        pltpu.SemaphoreType.DMA((22,)), pltpu.SemaphoreType.DMA((22,))],
+        compiler_params=pltpu.CompilerParams(collective_id=2, has_side_effects=True),
+    )(x)
+
 
 CLUSTER_TALLY = 32
 
@@ -64,13 +446,19 @@
     return joined.reshape(-1, joined.shape[-1])
 
 
+def pair_sum(first, second):
+    rows = jnp.concatenate([first[None], second[None], jnp.zeros((6, 384), jnp.float32)], 0)
+    total = all_sum(rows)
+    return total[0], total[1]
+
+
 def body(video, down_weight, conv_weight, norm_gain_vector, norm_shift_vector, output_gradient):
     chans = video.shape[3]
     cluster_width = chans // CLUSTER_TALLY
     frame_count = lax.axis_size("frame")
     row_count = lax.axis_size("row")
     devices = frame_count * row_count
-    kernel_full = lax.all_gather(conv_weight, ("frame", "row"), axis=0, tiled=True)
+    kernel_full = gather_weights(conv_weight)
     before = from_behind(video[1:2], "frame", 1)
     stacked = jnp.concatenate([before[0], video[0], video[1]], -1)
     slab_rows, slab_cols = (stacked.shape[0], stacked.shape[1])
@@ -80,12 +468,9 @@
     halved_clip = lax.all_to_all(down_frame, "frame", split_axis=2, concat_axis=0, tiled=True)
     halve_frames_routine = halved_clip.astype(jnp.float32)
     frames, height, width = (halved_clip.shape[0], halved_clip.shape[1], halved_clip.shape[2])
-    total_sum, total_square = lax.psum(
-        (
-            jnp.sum(halve_frames_routine, (0, 1, 2)),
-            jnp.sum(halve_frames_routine * halve_frames_routine, (0, 1, 2)),
-        ),
-        ("frame", "row"),
+    total_sum, total_square = pair_sum(
+        jnp.sum(halve_frames_routine, (0, 1, 2)),
+        jnp.sum(halve_frames_routine * halve_frames_routine, (0, 1, 2)),
     )
     element_tally = frames * height * width * devices * cluster_width
     cluster_average = total_sum.reshape(CLUSTER_TALLY, cluster_width).sum(1) / element_tally
@@ -105,9 +490,7 @@
     encoded_local = (halve_frames_routine + residual_path).astype(jnp.bfloat16)
     grad_flat = output_gradient.reshape(-1, chans)
     piece = tap_rows
-    grad_conv = lax.psum_scatter(
-        contract_rows(piece, grad_flat), ("frame", "row"), scatter_dimension=0, tiled=True
-    )
+    conv_part = contract_rows(piece, grad_flat)
     grad_border = extended(output_gradient, (("frame", 2), ("row", 1)), 1)
     grad_padded = jnp.pad(grad_border, ((0, 2), (0, 0), (0, 0), (0, 0)))
     flipped = kernel_full.reshape(27, chans, chans).transpose(0, 2, 1).reshape(27 * chans, chans)
@@ -119,12 +502,9 @@
     before_nonlinearity_cotangent = activation_cotangent.reshape(
         halve_frames_routine.shape
     ) * swish_derivative(before_nonlinearity)
-    grad_shift, gain_gradient = lax.psum(
-        (
-            jnp.sum(before_nonlinearity_cotangent, (0, 1, 2)),
-            jnp.sum(before_nonlinearity_cotangent * standardized_source, (0, 1, 2)),
-        ),
-        ("frame", "row"),
+    grad_shift, gain_gradient = pair_sum(
+        jnp.sum(before_nonlinearity_cotangent, (0, 1, 2)),
+        jnp.sum(before_nonlinearity_cotangent * standardized_source, (0, 1, 2)),
     )
     first_moment_mean = jnp.repeat(
         (norm_gain_vector * grad_shift).reshape(CLUSTER_TALLY, cluster_width).sum(1)
@@ -155,9 +535,8 @@
     )
     grad_video = jnp.stack([even_grad, odd_grad], 0).astype(jnp.bfloat16).reshape(video.shape)
     piece = flat_in
-    grad_down = lax.psum_scatter(
-        contract_rows(piece, latent_flat), ("frame", "row"), scatter_dimension=0, tiled=True
-    )
+    both = scatter_sum(conv_part, contract_rows(piece, latent_flat))
+    grad_conv, grad_down = both[:81], both[81:90]
     return (encoded_local, grad_video, grad_conv, grad_down, gain_gradient, grad_shift)
 
 

time: 1070 us -> 246 us (0.23)
  blocking collectives: 526 us -> 0 us
  waiting for transfers between devices: 299 us -> 9.81 us
  Pallas kernels: 0 us -> 135 us
  starting transfers between devices: 115 us -> 38.7 us
  local copies, waits for them, and re-layouts: 69 us -> 28.3 us
  between operations: 15 us -> 1.26 us
    unnamed x1 -> x0, blocking collectives: 389 us -> none
    all_gather x1 -> x0, waiting for transfers between devices: 202 us -> none  [body(): lax.all_gather(conv_weight, ('frame', 'row'), axis=0, tiled=True)]
    psum x2 -> x0, blocking collectives: 137 us -> none  [the longest x1 69.3 us: body(): lax.psum((jnp.sum(halve_frames_routine, (0, 1, 2)), jnp.sum(halve_frames_...]
    pallas_call x0 -> x4, Pallas kernels: none -> 135 us  [the longest x1 56.1 us: scatter_sum(): pl.pallas_call(functools.partial(scatter_kernel, BLOCK), out_shape=jax.Sh...]
    unnamed x23 -> x0, waiting for transfers between devices: 88.3 us -> none
    unnamed x21 -> x0, starting transfers between devices: 71.1 us -> none
    unnamed x101 -> x66, local copies, waits for them, and re-layouts: 41.9 us -> 5.34 us
  transfers between devices with their start and end apart: 34 -> 12, of which waited for: 7 -> 4; matrix products, arithmetic and copies ran while one was open for 43% -> 13% of each run, Pallas kernels for 0% -> 21%
where the time goes in v1:
time: 246 us; the launch traced here: 242 us
  Pallas kernels  135 us (55%)
  starting transfers between devices  38.7 us (16%)
  local copies, waits for them, and re-layouts  28.3 us (12%)
  matrix products  21 us (9%)
  waiting for transfers between devices  9.81 us (4%)
  other arithmetic  7.07 us (3%)
    pallas_call x1, Pallas kernels, scatter_sum(): pl.pallas_call(functools.partial(scatter_kernel, BLOCK), out_shape=jax.Sh...  56.1 us
    pallas_call x1, Pallas kernels, gather_weights(): pl.pallas_call(gather_kernel, out_shape=jax.ShapeDtypeStruct((10368, 384)...  51.9 us
    pallas_call x2, Pallas kernels, all_sum(): pl.pallas_call(sum_kernel, out_shape=jax.ShapeDtypeStruct((8, 384), jnp.f...  27.5 us
    ppermute x4, starting transfers between devices, extended(): lax.ppermute(lax.slice_in_dim(block, block.shape[dim] - width, None, axis...  15.2 us
    transpose x1, local copies, waits for them, and re-layouts, body(): kernel_full.reshape(27, chans, chans).transpose(0, 2, 1)  11.6 us
    dot_general x2, matrix products, contract_rows(): lax.dot_general(left, right, (((0,), (0,)), ((), ())), preferred_element_...  8.89 us
    all_to_all x1, starting transfers between devices, body(): lax.all_to_all(latent_gradient, 'frame', split_axis=0, concat_axis=2, til...  8.38 us
    dot_general x1, matrix products, body(): jnp.dot(backward_taps(grad_padded, frames, height, width), flipped, prefe...  7.21 us
  transfers between devices with their start and end apart: 12, of which 4 were waited for; matrix products, arithmetic and copies ran while one was open for 13% of the time, Pallas kernels for 21%

profile of v1, /device:TPU:0, one launch (start us, length us, event | category | flops | bytes accessed | tf_op | source)
XLA Modules:
  0.0 241.6 jit_solution(2036537098419259758)
XLA Ops:
  0.6 1.1 fusion.48
  1.7 1.3 collective-permute-start.6
  3.0 3.0 %collective-permute-start.5 = (bf16[16,2,1,384]{3,2,1,0:T(2,128)(2,1)S(1)}, bf16[16,2,1,384]{3,2,1,0:T(2,128)(2,1)S(1)}, u32[]{:S(2)}, u32[]{:S(2)}) collective-permute-start(bf16[16,2,1,384]{3,2,1,0:T(2,128)(2,1)S(1)} %get-tuple-element.26), channel_id=1, source_target_pairs={{0,8},{8,16},{16,24},{24,32},{32,40},{40,48},{48,56},{56,64},{64,7... | collective-permute-start | bytes 73736 | tf_op jit(solution)/shard_map/ppermute | solution.py:402
  6.1 0.9 collective-permute-done.5
  6.9 1.1 pad_maximum_fusion.4
  8.1 1.3 collective-permute-start.8
  9.4 4.6 %collective-permute-start.7 = (bf16[16,1,10,384]{3,2,1,0:T(8,128)(2,1)S(1)}, bf16[16,1,10,384]{3,2,1,0:T(8,128)(2,1)S(1)}, u32[]{:S(2)}, u32[]{:S(2)}) collective-permute-start(bf16[16,1,10,384]{3,2,1,0:T(8,128)(2,1)S(1)} %get-tuple-element.14), channel_id=1, source_target_pairs={{0,1},{1,2},{2,3},{3,4},{4,5},{5,6},{6,7},{8,9},{9,10},{10,11},{11... | collective-permute-start | bytes 368648 | tf_op jit(solution)/shard_map/ppermute | solution.py:402
  14.0 1.1 fusion.47
  15.1 3.3 %collective-permute-start = (bf16[1,2,128,384]{3,2,1,0:T(8,128)(2,1)S(1)}, bf16[1,2,128,384]{3,2,1,0:T(8,128)(2,1)S(1)}, u32[]{:S(2)}, u32[]{:S(2)}) collective-permute-start(bf16[1,2,128,384]{3,2,1,0:T(8,128)(2,1)S(1)} %get-tuple-element.19), channel_id=1, source_target_pairs={{0,8},{8,16},{16,24},{24,32},{32,40},{40,48},{48,56},{56,64},{64,7... | collective-permute-start | bytes 589832 | tf_op jit(solution)/shard_map/ppermute | solution.py:394
  18.3 1.5 bitcast_bitcast_fusion.w_ref
  19.9 51.9 %shard_map.110 = bf16[10368,384]{1,0:T(8,128)(2,1)} custom-call(bf16[3,96,128]{2,1,0:T(8,128)(2,1)} %bitcast_bitcast_fusion.w_ref), custom_call_target="tpu_custom_call" | custom-call | tf_op jit(solution)/shard_map/pallas_call | solution.py:160
  71.8 11.6 %copy.27 = bf16[27,384,384]{2,1,0:T(8,128)(2,1)} copy(bf16[27,384,384]{1,2,0:T(8,128)(2,1)} %bitcast.86) | data formatting | bytes 15925248 | tf_op jit(solution)/shard_map/transpose | solution.py:496
  83.4 0.3 fusion.25
  84.9 0.5 maximum_maximum_fusion.1
  86.1 2.3 copy-done.5
  88.5 0.5 convolution_convert_fusion.1
  88.9 0.9 copy.23
  89.8 5.4 %all-to-all-start = ((bf16[1,2,128,384]{3,1,0,2:T(2,128)(2,1)}), bf16[1,2,128,384]{3,1,0,2:T(2,128)(2,1)S(1)}, u32[]{:S(2)}, u32[]{:S(2)}) async-start(bf16[1,2,128,384]{3,1,0,2:T(2,128)(2,1)} %copy.23), calls=%async_computation | async-start | bytes 393216 | tf_op jit(solution)/shard_map/all_to_all | solution.py:468
  95.2 0.7 slice_dynamic-update-slice_fusion
  96.0 6.6 %all-to-all-done = bf16[1,2,128,384]{3,1,0,2:T(2,128)(2,1)S(1)} async-done(((bf16[1,2,128,384]{3,1,0,2:T(2,128)(2,1)}), bf16[1,2,128,384]{3,1,0,2:T(2,128)(2,1)S(1)}, u32[]{:S(2)}, u32[]{:S(2)}) %all-to-all-start) | async-done | bytes 196640 | tf_op jit(solution)/shard_map/all_to_all | solution.py:468
  102.7 0.7 maximum_maximum_fusion.2.x_ref
  103.4 12.9 %shard_map.109 = f32[8,384]{1,0:T(8,128)} custom-call(f32[8,384]{1,0:T(8,128)} %maximum_maximum_fusion.2.x_ref), custom_call_target="tpu_custom_call" | custom-call | tf_op jit(solution)/shard_map/pallas_call | solution.py:377
  116.3 0.8 slice_reduce_fusion.3
  117.9 7.2 %fusion.44 = (f32[384]{0:T(512)S(1)}, f32[384]{0:T(512)S(1)}, f32[16,2,8,384]{3,2,1,0:T(8,128)S(1)}) fusion(f32[384]{0:T(512)S(1)} %mul.70, f32[384]{0:T(512)S(1)} %sub.29, f32[384]{0:T(512)S(1)} %copy-done.6, f32[384]{0:T(512)S(1)} %copy-done.2, bf16[16,2,8,10368]{3,2,1,0:T(8,128)(2,1)} %slice_dynamic-update-slice_fusion, ...), kind=kOutput, calls=%fused_computation.131 | convolution fusion | flops 2040003840 | bytes 13870080 | tf_op jit(solution)/shard_map/dot_general | solution.py:497
  125.2 0.7 maximum_maximum_fusion.3.x_ref
  125.9 14.6 %shard_map.111 = f32[8,384]{1,0:T(8,128)} custom-call(f32[8,384]{1,0:T(8,128)} %maximum_maximum_fusion.3.x_ref), custom_call_target="tpu_custom_call" | custom-call | tf_op jit(solution)/shard_map/pallas_call | solution.py:377
  140.5 0.8 slice_reduce_fusion.1
  142.2 0.9 add_convert_fusion
  143.2 1.3 collective-permute-start.2
  144.5 3.0 %collective-permute-start.1 = (bf16[16,2,1,384]{3,2,1,0:T(2,128)(2,1)S(1)}, bf16[16,2,1,384]{3,2,1,0:T(2,128)(2,1)S(1)}, u32[]{:S(2)}, u32[]{:S(2)}) collective-permute-start(bf16[16,2,1,384]{3,2,1,0:T(2,128)(2,1)S(1)} %get-tuple-element.28), channel_id=1, source_target_pairs={{0,8},{8,16},{16,24},{24,32},{32,40},{40,48},{48,56},{56,64},{64,7... | collective-permute-start | bytes 73736 | tf_op jit(solution)/shard_map/ppermute | solution.py:402
  147.5 0.9 collective-permute-done.1
  148.6 1.3 collective-permute-start.4
  149.9 4.6 %collective-permute-start.3 = (bf16[16,1,10,384]{3,2,1,0:T(8,128)(2,1)S(1)}, bf16[16,1,10,384]{3,2,1,0:T(8,128)(2,1)S(1)}, u32[]{:S(2)}, u32[]{:S(2)}) collective-permute-start(bf16[16,1,10,384]{3,2,1,0:T(8,128)(2,1)S(1)} %get-tuple-element.16), channel_id=1, source_target_pairs={{0,1},{1,2},{2,3},{3,4},{4,5},{5,6},{6,7},{8,9},{9,10},{10,11},{11... | collective-permute-start | bytes 368648 | tf_op jit(solution)/shard_map/ppermute | solution.py:402
  154.5 8.4 %all-to-all-start.1 = ((bf16[16,2,8,384]{3,2,1,0:T(8,128)(2,1)}), bf16[16,2,8,384]{3,2,1,0:T(8,128)(2,1)S(1)}, u32[]{:S(2)}, u32[]{:S(2)}) async-start(bf16[16,2,8,384]{3,2,1,0:T(8,128)(2,1)} %get-tuple-element.12), calls=%async_computation.1 | async-start | bytes 393216 | tf_op jit(solution)/shard_map/all_to_all | solution.py:528
  162.9 0.3 fusion.21
  164.4 0.5 pad_maximum_fusion.1
  165.6 7.2 %convolution_bitcast_fusion.gc_ref = f32[10368,384]{1,0:T(8,128)} fusion(bf16[16,2,8,10368]{3,2,1,0:T(8,128)(2,1)S(1)} %slice_dynamic-update-slice_fusion.24, bf16[16,2,8,384]{3,2,1,0:T(8,128)(2,1)S(1)} %copy-done), kind=kOutput, calls=%fused_computation | convolution fusion | flops 2038431744 | bytes 21430272 | tf_op jit(solution)/shard_map/dot_general | solution.py:416
  172.8 3.6 %fusion.16 = bf16[16,2,8,384]{3,2,1,0:T(8,128)(2,1)} fusion(bf16[16,2,8,10368]{3,2,1,0:T(8,128)(2,1)S(1)} %slice_dynamic-update-slice_fusion.24, bf16[10368,384]{1,0:T(8,128)(2,1)S(1)} %bitcast.88, bf16[1,2,128,384]{3,1,0,2:T(2,128)(2,1)S(1)} %all-to-all-done), kind=kOutput, calls=%fused_computation.21 | convolution fusion | flops 2038726656 | bytes 13664256 | tf_op jit(solution)/shard_map/dot_general | solution.py:487
  176.5 1.7 fusion.35.gd_ref
  178.2 56.1 %shard_map.112 = f32[96,384]{1,0:T(8,128)} custom-call(f32[10368,384]{1,0:T(8,128)} %convolution_bitcast_fusion.gc_ref, f32[1152,384]{1,0:T(8,128)} %fusion.35.gd_ref), custom_call_target="tpu_custom_call" | custom-call | tf_op jit(solution)/shard_map/pallas_call | solution.py:323
  234.2 1.6 slice.325
  235.8 1.3 slice.326
  237.1 1.3 collective-permute-start.9
  238.4 0.3 fusion.19
  238.7 0.3 fusion.32
  239.0 1.5 collective-permute-done.9
  240.5 0.3 fusion.15
  240.8 0.8 pad_maximum_fusion.5
  (112 shorter events, 5.8 us)
Async XLA Ops:
  1.7 4.3 %collective-permute-start.6 = (bf16[16,2,1,384]{3,2,1,0:T(2,128)(2,1)S(1)}, bf16[16,2,1,384]{3,2,1,0:T(2,128)(2,1)S(1)}, u32[]{:S(2)}, u32[]{:S(2)}) collective-permute-start(bf16[16,2,1,384]{3,2,1,0:T(2,128)(2,1)S(1)} %get-tuple-element.27), channel_id=1, source_target_pairs={{8,0},{16,8},{24,16},{32,24},{40,32},{48,40},{56,48},{64,56},{72,6... | collective-permute-start | bytes 73736 | tf_op jit(solution)/shard_map/ppermute | solution.py:405
  3.0 3.9 %collective-permute-start.5 = (bf16[16,2,1,384]{3,2,1,0:T(2,128)(2,1)S(1)}, bf16[16,2,1,384]{3,2,1,0:T(2,128)(2,1)S(1)}, u32[]{:S(2)}, u32[]{:S(2)}) collective-permute-start(bf16[16,2,1,384]{3,2,1,0:T(2,128)(2,1)S(1)} %get-tuple-element.26), channel_id=1, source_target_pairs={{0,8},{8,16},{16,24},{24,32},{32,40},{40,48},{48,56},{56,64},{64,7... | collective-permute-start | bytes 73736 | tf_op jit(solution)/shard_map/ppermute | solution.py:402
  8.1 75.3 %collective-permute-start.8 = (bf16[16,1,10,384]{3,2,1,0:T(8,128)(2,1)S(1)}, bf16[16,1,10,384]{3,2,1,0:T(8,128)(2,1)S(1)}, u32[]{:S(2)}, u32[]{:S(2)}) collective-permute-start(bf16[16,1,10,384]{3,2,1,0:T(8,128)(2,1)S(1)} %get-tuple-element.15), channel_id=1, source_target_pairs={{1,0},{2,1},{3,2},{4,3},{5,4},{6,5},{7,6},{9,8},{10,9},{11,10},{12... | collective-permute-start | bytes 368648 | tf_op jit(solution)/shard_map/ppermute | solution.py:405
  9.4 74.0 %collective-permute-start.7 = (bf16[16,1,10,384]{3,2,1,0:T(8,128)(2,1)S(1)}, bf16[16,1,10,384]{3,2,1,0:T(8,128)(2,1)S(1)}, u32[]{:S(2)}, u32[]{:S(2)}) collective-permute-start(bf16[16,1,10,384]{3,2,1,0:T(8,128)(2,1)S(1)} %get-tuple-element.14), channel_id=1, source_target_pairs={{0,1},{1,2},{2,3},{3,4},{4,5},{5,6},{6,7},{8,9},{9,10},{10,11},{11... | collective-permute-start | bytes 368648 | tf_op jit(solution)/shard_map/ppermute | solution.py:402
  15.1 71.0 %collective-permute-start = (bf16[1,2,128,384]{3,2,1,0:T(8,128)(2,1)S(1)}, bf16[1,2,128,384]{3,2,1,0:T(8,128)(2,1)S(1)}, u32[]{:S(2)}, u32[]{:S(2)}) collective-permute-start(bf16[1,2,128,384]{3,2,1,0:T(8,128)(2,1)S(1)} %get-tuple-element.19), channel_id=1, source_target_pairs={{0,8},{8,16},{16,24},{24,32},{32,40},{40,48},{48,56},{56,64},{64,7... | collective-permute-start | bytes 589832 | tf_op jit(solution)/shard_map/ppermute | solution.py:394
  71.7 11.7 %copy-start = (bf16[16,2,8,384]{3,2,1,0:T(8,128)(2,1)S(1)}, bf16[16,2,8,384]{3,2,1,0:T(8,128)(2,1)}, u32[]{:S(2)}) copy-start(bf16[16,2,8,384]{3,2,1,0:T(8,128)(2,1)} %param.11) | copy-start | bytes 589828
  84.0 4.5 %copy-start.1 = (bf16[1152,384]{1,0:T(8,128)(2,1)S(1)}, bf16[1152,384]{1,0:T(8,128)(2,1)}, u32[]{:S(2)}) copy-start(bf16[1152,384]{1,0:T(8,128)(2,1)} %param.7) | copy-start | bytes 2654212
  84.8 33.1 %copy-start.2 = (f32[384]{0:T(512)S(1)}, f32[384]{0:T(512)}, u32[]{:S(2)}) copy-start(f32[384]{0:T(512)} %param.9) | copy-start | bytes 4612
  84.8 33.1 %copy-start.6 = (f32[384]{0:T(512)S(1)}, f32[384]{0:T(512)}, u32[]{:S(2)}) copy-start(f32[384]{0:T(512)} %param.10) | copy-start | bytes 4612
  86.1 2.4 copy-start.5
  89.8 12.8 %all-to-all-start = ((bf16[1,2,128,384]{3,1,0,2:T(2,128)(2,1)}), bf16[1,2,128,384]{3,1,0,2:T(2,128)(2,1)S(1)}, u32[]{:S(2)}, u32[]{:S(2)}) async-start(bf16[1,2,128,384]{3,1,0,2:T(2,128)(2,1)} %copy.23), calls=%async_computation | async-start | bytes 393216 | tf_op jit(solution)/shard_map/all_to_all | solution.py:468
  141.3 22.9 %copy-start.3 = (f32[384]{0:T(512)}, f32[384]{0:T(512)S(1)}, u32[]{:S(2)}) copy-start(f32[384]{0:T(512)S(1)} %get-tuple-element.8) | copy-start | bytes 4612
  141.3 22.9 %copy-start.4 = (f32[384]{0:T(512)}, f32[384]{0:T(512)S(1)}, u32[]{:S(2)}) copy-start(f32[384]{0:T(512)S(1)} %get-tuple-element.9) | copy-start | bytes 4612
  143.2 4.3 %collective-permute-start.2 = (bf16[16,2,1,384]{3,2,1,0:T(2,128)(2,1)S(1)}, bf16[16,2,1,384]{3,2,1,0:T(2,128)(2,1)S(1)}, u32[]{:S(2)}, u32[]{:S(2)}) collective-permute-start(bf16[16,2,1,384]{3,2,1,0:T(2,128)(2,1)S(1)} %get-tuple-element.29), channel_id=1, source_target_pairs={{8,0},{16,8},{24,16},{32,24},{40,32},{48,40},{56,48},{64,56},{72,6... | collective-permute-start | bytes 73736 | tf_op jit(solution)/shard_map/ppermute | solution.py:405
  144.5 3.9 %collective-permute-start.1 = (bf16[16,2,1,384]{3,2,1,0:T(2,128)(2,1)S(1)}, bf16[16,2,1,384]{3,2,1,0:T(2,128)(2,1)S(1)}, u32[]{:S(2)}, u32[]{:S(2)}) collective-permute-start(bf16[16,2,1,384]{3,2,1,0:T(2,128)(2,1)S(1)} %get-tuple-element.28), channel_id=1, source_target_pairs={{0,8},{8,16},{16,24},{24,32},{32,40},{40,48},{48,56},{56,64},{64,7... | collective-permute-start | bytes 73736 | tf_op jit(solution)/shard_map/ppermute | solution.py:402
  148.6 14.3 %collective-permute-start.4 = (bf16[16,1,10,384]{3,2,1,0:T(8,128)(2,1)S(1)}, bf16[16,1,10,384]{3,2,1,0:T(8,128)(2,1)S(1)}, u32[]{:S(2)}, u32[]{:S(2)}) collective-permute-start(bf16[16,1,10,384]{3,2,1,0:T(8,128)(2,1)S(1)} %get-tuple-element.17), channel_id=1, source_target_pairs={{1,0},{2,1},{3,2},{4,3},{5,4},{6,5},{7,6},{9,8},{10,9},{11,10},{12... | collective-permute-start | bytes 368648 | tf_op jit(solution)/shard_map/ppermute | solution.py:405
  149.9 13.0 %collective-permute-start.3 = (bf16[16,1,10,384]{3,2,1,0:T(8,128)(2,1)S(1)}, bf16[16,1,10,384]{3,2,1,0:T(8,128)(2,1)S(1)}, u32[]{:S(2)}, u32[]{:S(2)}) collective-permute-start(bf16[16,1,10,384]{3,2,1,0:T(8,128)(2,1)S(1)} %get-tuple-element.16), channel_id=1, source_target_pairs={{0,1},{1,2},{2,3},{3,4},{4,5},{5,6},{6,7},{8,9},{9,10},{10,11},{11... | collective-permute-start | bytes 368648 | tf_op jit(solution)/shard_map/ppermute | solution.py:402
  154.5 21.9 %all-to-all-start.1 = ((bf16[16,2,8,384]{3,2,1,0:T(8,128)(2,1)}), bf16[16,2,8,384]{3,2,1,0:T(8,128)(2,1)S(1)}, u32[]{:S(2)}, u32[]{:S(2)}) async-start(bf16[16,2,8,384]{3,2,1,0:T(8,128)(2,1)} %get-tuple-element.12), calls=%async_computation.1 | async-start | bytes 393216 | tf_op jit(solution)/shard_map/all_to_all | solution.py:528
  164.9 7.9 %slice-start = ((s8[7962624]{0:T(1024)(128)(4,1)}), s8[4194304]{0:T(1024)(128)(4,1)S(1)}, s32[]{:S(2)}) async-start(s8[7962624]{0:T(1024)(128)(4,1)} %bitcast.87), calls=%async_computation.2 | async-start | bytes 8388608
  165.6 7.2 %slice-start.1 = ((s8[7962624]{0:T(1024)(128)(4,1)}), s8[3768320]{0:T(1024)(128)(4,1)S(1)}, s32[]{:S(2)}) async-start(s8[7962624]{0:T(1024)(128)(4,1)} %bitcast.87), calls=%async_computation.3 | async-start | bytes 7536640
  237.1 3.3 %collective-permute-start.9 = (bf16[1,2,128,384]{3,2,1,0:T(8,128)(2,1)S(1)}, bf16[1,2,128,384]{3,2,1,0:T(8,128)(2,1)S(1)}, u32[]{:S(2)}, u32[]{:S(2)}) collective-permute-start(bf16[1,2,128,384]{3,2,1,0:T(8,128)(2,1)S(1)} %get-tuple-element.24), channel_id=1, source_target_pairs={{8,0},{16,8},{24,16},{32,24},{40,32},{48,40},{56,48},{64,56},{72,6... | collective-permute-start | bytes 589832 | tf_op jit(solution)/shard_map/ppermute | solution.py:394

commit v2 on v1

v2 whole, which is shorter than its diff:
```python
import functools
import jax
import jax.numpy as jnp
from jax import lax
from jax.experimental import pallas as pl
from jax.experimental.pallas import tpu as pltpu
from jax.sharding import PartitionSpec as P

MESH = pl.DeviceIdType.MESH
AXES = "xyz"
ORDERS = ("xyz", "yzx", "zxy")
BLOCK = 96
LANES = 128


def position():
    f, r = lax.axis_index("frame"), lax.axis_index("row")
    y = lax.div(r, 4) * 2 + lax.div(f, 8)
    pos = {"x": lax.rem(r, 4), "y": y, "z": lax.rem(lax.div(f, 2), 4)}
    return f, r, pos, lax.rem(f, 2)


def device_at(pos, core):
    frame = lax.rem(pos["y"], 2) * 8 + pos["z"] * 2 + core
    row = lax.div(pos["y"], 2) * 4 + pos["x"]
    return (frame, row)


def shifted(pos, axis, steps):
    moved = dict(pos)
    moved[axis] = lax.rem(pos[axis] + (steps + 4), 4)
    return moved


def chip_neighbours(pos, core):
    near = [device_at(shifted(pos, axis, s), core) for axis in AXES for s in (1, -1)]
    return near + [device_at(pos, 1 - core)]


def greet(devices):
    barrier = pltpu.get_barrier_semaphore()
    for device in devices:
        pl.semaphore_signal(barrier, inc=1, device_id=device, device_id_type=MESH)
    pl.semaphore_wait(barrier, len(devices))


def remote(src, dst, sems, index, device):
    return pltpu.make_async_remote_copy(
        src_ref=src,
        dst_ref=dst,
        send_sem=sems[0].at[index],
        recv_sem=sems[1].at[index],
        device_id=device,
        device_id_type=MESH,
    )


GATHER_COPIES = 16


def gather_steps(pos, core, order, buf, sems, base):
    a, b, c = order
    ca, cb, cc = pos[a], pos[b], pos[c]
    sent = []

    def start(src, dst, device):
        op = remote(src, dst, sems, base + len(sent), device)
        op.start()
        sent.append(op)
        return op

    whole = {
        c: lambda i: buf.at[core, ca, cb, i],
        b: lambda i: buf.at[core, ca, i],
        a: lambda i: buf.at[core, i],
    }
    half = BLOCK // 2
    parts = {
        c: lambda i, h: buf.at[core, ca, cb, i, pl.ds(h * half, half)],
        b: lambda i, h: buf.at[core, ca, i, pl.ds(2 * h, 2)],
        a: lambda i, h: buf.at[core, i, pl.ds(2 * h, 2)],
    }
    other = device_at(pos, 1 - core)
    for axis in (c, b, a):
        me = pos[axis]
        up, down = shifted(pos, axis, 1), shifted(pos, axis, -1)
        mine, one, ref = whole[axis](me), whole[axis], parts[axis]
        first = start(mine, mine, device_at(up, core))
        second = start(mine, mine, device_at(down, core))
        if axis == a:
            start(mine, mine, other)
        yield
        first.wait_recv()
        third = start(ref(down[axis], 0), ref(down[axis], 0), device_at(up, core))
        if axis == a:
            start(one(down[axis]), one(down[axis]), other)
        second.wait_recv()
        fourth = start(ref(up[axis], 1), ref(up[axis], 1), device_at(down, core))
        if axis == a:
            start(one(up[axis]), one(up[axis]), other)
        yield
        third.wait_recv()
        fourth.wait_recv()
    far = shifted(pos, a, 2)[a]
    start(buf.at[core, far], buf.at[core, far], other)
    yield
    for k, op in enumerate(sent):
        if k in (10, 12, 14, 15):
            op.wait_recv()
        op.wait_send()


def interleave(steps):
    steps = list(steps)
    while steps:
        left = []
        for step in steps:
            try:
                next(step)
                left.append(step)
            except StopIteration:
                pass
        steps = left


SCATTER_COPIES = 16


def add_into(count, target, terms):
    def step(i, _):
        total = terms[0](i).astype(jnp.float32)
        for term in terms[1:]:
            total = total + term(i).astype(jnp.float32)
        target(i, total)
        return 0

    lax.fori_loop(0, count, step, 0)


def scatter_steps(pos, core, order, rows, piles, got, near, q, near_q, u, near_u, sems, base, out):
    a, b, c = order
    ca, cb, cc = pos[a], pos[b], pos[c]
    half = rows // 2
    sent = []

    def start(src, dst, device):
        op = remote(src, dst, sems, base + len(sent), device)
        op.start()
        sent.append(op)
        return op

    def toward(axis, steps):
        return device_at(shifted(pos, axis, steps), core)

    def at(axis, steps):
        return shifted(pos, axis, steps)[axis]

    other = device_at(pos, 1 - core)
    far, up, down = at(a, 2), at(a, 1), at(a, -1)
    swaps = [start(piles.at[1 - core, i], got.at[i], other) for i in (far, up, down, ca)]
    yield

    def store(i):
        def put(k, total):
            piles[core, i, k] = total.astype(jnp.bfloat16)
        return put

    def pair(i, first=0):
        return [lambda k: piles[core, i, k + first], lambda k: got[i, k + first]]

    near_a, near_b, near_c, near_d = near
    swaps[0].wait_recv()
    add_into(4, store(far), pair(far))
    op_a = start(piles.at[core, far, pl.ds(0, 2)], near_a, toward(a, 1))
    op_b = start(piles.at[core, far, pl.ds(2, 2)], near_b, toward(a, -1))
    yield
    swaps[1].wait_recv()
    op_a.wait_recv()
    add_into(2, store(up), pair(up) + [lambda k: near_a[k]])
    add_into(2, lambda k, total: store(up)(k + 2, total), pair(up, 2))
    op_c = start(piles.at[core, up], near_c, toward(a, 1))
    swaps[2].wait_recv()
    op_b.wait_recv()
    add_into(2, store(down), pair(down))
    add_into(2, lambda k, total: store(down)(k + 2, total), pair(down, 2) + [lambda k: near_b[k]])
    op_d = start(piles.at[core, down], near_d, toward(a, -1))
    yield
    swaps[3].wait_recv()
    op_c.wait_recv()
    op_d.wait_recv()

    def put_q(k, total):
        q[k] = total

    add_into(4, put_q, pair(ca) + [lambda k: near_c[k], lambda k: near_d[k]])
    for axis, v, near_v, low, high, lower, upper in (
        (b, q, near_q, lambda i: q.at[i, pl.ds(0, 2)], lambda i: q.at[i, pl.ds(2, 2)],
         pl.ds(0, 2), pl.ds(2, 2)),
        (c, u, near_u, lambda i: u.at[i, pl.ds(0, half)], lambda i: u.at[i, pl.ds(half, half)],
         pl.ds(0, half), pl.ds(half, half)),
    ):
        far, up, down, me = at(axis, 2), at(axis, 1), at(axis, -1), pos[axis]
        near_a, near_b, near_c, near_d = near_v
        op_a = start(low(far), near_a, toward(axis, 1))
        op_b = start(high(far), near_b, toward(axis, -1))
        yield
        op_a.wait_recv()
        v[up, lower] = v[up, lower] + near_a[...]
        op_c = start(v.at[up], near_c, toward(axis, 1))
        op_b.wait_recv()
        v[down, upper] = v[down, upper] + near_b[...]
        op_d = start(v.at[down], near_d, toward(axis, -1))
        yield
        op_c.wait_recv()
        op_d.wait_recv()
        total = v[me] + near_c[...] + near_d[...]
        if axis == b:
            u[...] = total
        else:
            out(total)
    yield
    for op in sent:
        op.wait_send()


def scatter_scratch(rows):
    def bf(*lead):
        return pltpu.VMEM(lead + (rows, LANES), jnp.bfloat16)

    def f32(*lead):
        return pltpu.VMEM(lead + (rows, LANES), jnp.float32)

    half = pltpu.VMEM((rows // 2, LANES), jnp.float32)
    one = [bf(2, 4, 4, 4), bf(4, 4, 4), bf(2, 4), bf(2, 4), bf(4, 4), bf(4, 4), f32(4, 4),
           f32(2), f32(2), f32(4), f32(4), f32(4), half, half, f32(), f32()]
    return one


def sum_steps(f, r, x, done, row_in, frame_in, sems):
    row_in[r] = x
    ops = []
    for s in range(1, 8):
        peer = lax.rem(r + s, 8)
        op = remote(row_in.at[r], row_in.at[r], sems, s - 1, (f, peer))
        op.start()
        ops.append(op)
    yield
    for op in ops:
        op.wait_recv()
    total = row_in[0]
    for s in range(1, 8):
        total = total + row_in[s]
    frame_in[f] = total
    more = []
    for s in range(1, 16):
        peer = lax.rem(f + s, 16)
        op = remote(frame_in.at[f], frame_in.at[f], sems, 6 + s, (peer, r))
        op.start()
        more.append(op)
    yield
    for op in more:
        op.wait_recv()
    total = frame_in[0]
    for s in range(1, 16):
        total = total + frame_in[s]
    done(total)
    for op in ops + more:
        op.wait_send()


TAPS = 27
CHANS = 384
PIXELS = 256
TALLY = 16 * 16 * 128 * 12


def dot(left, right, contract=(1, 0)):
    return lax.dot_general(left, right, (((contract[0],), (contract[1],)), ((), ())),
                           preferred_element_type=jnp.float32)


def group_sum(rows, mask):
    return lax.dot_general(rows, mask, (((1,), (0,)), ((), ())),
                           precision=lax.Precision.HIGHEST, preferred_element_type=jnp.float32)


def only(condition, value):
    return jnp.where(condition, value, 0.0)


def load_rows(ref, start, count, stride):
    return jnp.concatenate([ref[j, pl.ds(start, count, stride=stride), :] for j in range(3)], 1)


def store_rows(ref, start, count, stride, value):
    for j in range(3):
        ref[j, pl.ds(start, count, stride=stride), :] = value[:, LANES * j : LANES * (j + 1)]


def halo_start(f, r, wide, lanes, out, into, sems):
    f_up, f_down = lax.rem(f + 1, 16), lax.rem(f + 15, 16)
    r_up, r_down = lax.rem(r + 1, 8), lax.rem(r + 7, 8)
    block = wide[...].reshape(16, 16, CHANS)
    store_rows(lanes, 0, PIXELS, 1, wide[...])
    ops = []

    def send(index, value, first, rows, device):
        out[first : first + rows, :] = value.astype(jnp.bfloat16)
        op = remote(out.at[pl.ds(first, rows)], into.at[pl.ds(first, rows)], sems, index, device)
        op.start()
        ops.append(op)

    send(0, block[:, 8:, :].reshape(128, CHANS), 0, 128, (f, r_up))
    send(1, block[:, :8, :].reshape(128, CHANS), 128, 128, (f, r_down))
    send(2, load_rows(lanes, 7, 32, 8), 256, 32, (f_up, r))
    send(3, load_rows(lanes, 0, 32, 8), 288, 32, (f_down, r))
    send(4, load_rows(lanes, 15, 16, 16), 320, 16, (f_up, r_up))
    send(5, load_rows(lanes, 8, 16, 16), 336, 16, (f_down, r_up))
    send(6, load_rows(lanes, 7, 16, 16), 352, 16, (f_up, r_down))
    send(7, load_rows(lanes, 0, 16, 16), 368, 16, (f_down, r_down))
    return ops


def halo_finish(f, r, ops, wide, into, ext, side, taps, first):
    for op in ops:
        op.wait_recv()
    top, bottom, left, right = r > 0, r < 7, f > 0, f < 15
    edge = into[...].astype(jnp.float32)
    middle = wide[...].reshape(16, 2, 8, CHANS)
    above = only(top, edge[0:128]).reshape(16, 1, 8, CHANS)
    below = only(bottom, edge[128:256]).reshape(16, 1, 8, CHANS)
    base = jnp.concatenate([above, middle, below], 1)
    store_rows(side, 0, 64, 1, jnp.concatenate(
        [only(left, edge[256:288]), only(right, edge[288:320])], 0))
    corner = {
        (0, 0): only(top & left, edge[320:336]),
        (0, 2): only(top & right, edge[336:352]),
        (3, 0): only(bottom & left, edge[352:368]),
        (3, 2): only(bottom & right, edge[368:384]),
    }
    for e in range(3):
        if e == 1:
            store_rows(ext, 0, 512, 1, base.reshape(512, CHANS))
        else:
            turned = pltpu.roll(base.reshape(64, 8, CHANS), 1 if e == 0 else 7, 1)
            store_rows(ext, 0, 512, 1, turned.reshape(512, CHANS))
            col = 0 if e == 0 else 7
            for i in range(4):
                if i in (0, 3):
                    value = corner[i, e]
                else:
                    value = load_rows(side, (0 if e == 0 else 32) + i - 1, 16, 2)
                store_rows(ext, 8 * i + col, 16, 32, value)
        full = load_rows(ext, 0, 512, 1).reshape(16, 32, CHANS)
        for b in range(3):
            rows = full[:, 8 * b : 8 * b + 16, :].reshape(PIXELS, CHANS)
            taps[3 * b + e, pl.ds(16 * first, PIXELS), :] = rows.astype(jnp.bfloat16)
    zeros = jnp.zeros((32, CHANS), jnp.bfloat16)
    for i in range(9):
        taps[i, pl.ds(0 if first else 256, 32), :] = zeros


def spread_start(f, r, out, into, width, sems):
    ops = []
    for s in range(1, 16):
        peer = lax.rem(f + s, 16)
        src = out.at[peer] if width == 1 else out.at[pl.ds(peer, width)]
        op = remote(src, into.at[f], sems, s - 1, (peer, r))
        op.start()
        ops.append(op)
    return ops


def pack_rows(source, first, groups, g0, size, rows, piles):
    def pack(n, _):
        g = g0 + n
        y_lo, z = lax.div(g, 4), lax.rem(g, 4)
        wide = source.at[pl.ds(pl.multiple_of(first + n * 16 * size, 8), 16 * size)]
        pad = jnp.zeros((rows - size, LANES), jnp.float32)
        for i in range(16):
            at = {"x": i % 4, "y": 2 * ((i // 4) % 2) + y_lo, "z": z}
            for j, (a, b, c) in enumerate(ORDERS):
                block = wide[size * i : size * i + size, LANES * j : LANES * (j + 1)]
                block = jnp.concatenate([block, pad], 0)
                piles[j][i // 8, at[a], at[b], at[c]] = block.astype(jnp.bfloat16)
        return 0

    lax.fori_loop(0, groups, pack, 0)


def section_kernel(video, wd, w_ref, gain_ref, shift_ref, og_ref, mask,
                   code_ref, gvideo_ref, gconv_ref, gdown_ref, ggain_ref, gshift_ref, *scratch):
    refs = list(scratch)

    def take(n):
        out = refs[:n]
        del refs[:n]
        return out

    bufs = take(3)
    big = [take(16) for _ in range(3)]
    small = [take(16) for _ in range(3)]
    (full, gbuf, wide, a_taps, g_taps, ext, side, lanes, h_out, h_in, g_out, g_in, before,
     d_out, d_in, l_out, l_in, row1, frame1, row2, frame2, act32, grad32) = take(23)
    sem = [(refs[2 * i], refs[2 * i + 1]) for i in range(len(refs) // 2)]
    s_gather, s_big, s_small, s_sum1, s_sum2, s_down, s_lat, s_act, s_grad, s_video = sem

    f, r, pos, core = position()
    peers = [(f, lax.rem(r + s, 8)) for s in range(1, 8)]
    peers += [(lax.rem(f + s, 16), r) for s in range(1, 16)]
    peers += [device_at(shifted(pos, "y", s), core) for s in (1, -1)]
    peers += [(lax.rem(f + s, 16), lax.rem(r + t, 8)) for s in (1, 15) for t in (1, 7)]
    greet(peers)
    waiting = []

    for j, (a, b, c) in enumerate(ORDERS):
        block = w_ref[:, LANES * j : LANES * (j + 1)].astype(jnp.float32)
        block = jnp.concatenate([block, jnp.zeros((BLOCK - 81, LANES), jnp.float32)], 0)
        bufs[j][core, pos[a], pos[b], pos[c]] = block.astype(jnp.bfloat16)
    weights = [gather_steps(pos, core, order, bufs[j], s_gather, j * GATHER_COPIES)
               for j, order in enumerate(ORDERS)]

    def advance(steps):
        for step in steps:
            next(step, None)

    ahead = remote(video.at[1], before, s_video, 0, (lax.rem(f + 1, 16), r))
    ahead.start()
    waiting.append(ahead)
    advance(weights)
    grad32[...] = og_ref[...].astype(jnp.float32).reshape(PIXELS, CHANS)
    grad_ops = halo_start(f, r, grad32, lanes, g_out, g_in, s_grad)
    waiting += grad_ops

    v0 = video[0].reshape(PIXELS, CHANS)
    v1 = video[1].reshape(PIXELS, CHANS)
    down = dot(v0, wd[CHANS : 2 * CHANS, :]) + dot(v1, wd[2 * CHANS :, :])
    ahead.wait_recv()
    vb = before[...].reshape(PIXELS, CHANS)
    down = down + only(f > 0, dot(vb, wd[:CHANS, :]))
    down = down.reshape(2, 16, 8, CHANS)
    d_out[...] = jnp.concatenate([down[0], down[1]], 1).astype(jnp.bfloat16)
    d_in[f] = d_out[f]
    down_ops = spread_start(f, r, d_out, d_in, 1, s_down)
    waiting += down_ops
    advance(weights)
    halo_finish(f, r, grad_ops, grad32, g_in, ext, side, g_taps, 0)
    for op in down_ops:
        op.wait_recv()
    latent = d_in[...].astype(jnp.float32).reshape(PIXELS, CHANS)

    def sum_rows(first, second):
        return jnp.concatenate([jnp.sum(first, 0, keepdims=True), jnp.sum(second, 0, keepdims=True),
                                jnp.zeros((6, CHANS), jnp.float32)], 0)

    total = []
    sums = sum_steps(f, r, sum_rows(latent, latent * latent), total.append, row1, frame1, s_sum1)
    next(sums)
    advance(weights)
    next(sums)
    advance(weights)
    next(sums, None)
    moments = group_sum(total[0], mask[...]) / TALLY
    mean = moments[0:1]
    rstd = lax.rsqrt(moments[1:2] - mean * mean + 1e-06)
    gain, shift = gain_ref[...], shift_ref[...]
    act32[...] = (latent - mean) * rstd
    xhat = act32[...]
    z = xhat * gain + shift
    grown = z / (1.0 + jnp.exp(-z))
    wide_act = gbuf.at[pl.ds(0, PIXELS)]
    wide_act[...] = grown
    act_ops = halo_start(f, r, wide_act, lanes, h_out, h_in, s_act)
    waiting += act_ops
    advance(weights)
    halo_finish(f, r, act_ops, wide_act, h_in, ext, side, a_taps, 2)

    cot = og_ref[...].reshape(PIXELS, CHANS)
    piles = [s[0] for s in big]
    for part in range(4):
        low, high = 2592 * part // CHANS, -(-2592 * (part + 1) // CHANS)

        def tap(n, _, low=low):
            k = n + low
            rows = a_taps[lax.rem(k, 9), pl.ds(pl.multiple_of(16 * lax.div(k, 9), 16), PIXELS), :]
            gbuf[pl.ds(pl.multiple_of(n * CHANS, CHANS), CHANS), :] = dot(rows, cot, (0, 0))
            return 0

        lax.fori_loop(0, high - low, tap, 0)
        pack_rows(gbuf, 2592 * part - CHANS * low, 2, 2 * part, 81, BLOCK, piles)
        if part == 1:
            advance(weights)

    def scatter(sets, rows, sems, out_ref):
        def run(j, order):
            s = sets[j]

            def out(total):
                out_ref[:, LANES * j : LANES * (j + 1)] = total[: out_ref.shape[0]]

            return scatter_steps(pos, core, order, rows, s[0], s[1], s[2:6], s[6], s[7:11],
                                 s[11], s[12:16], sems, j * SCATTER_COPIES, out)

        return [run(j, order) for j, order in enumerate(ORDERS)]

    conv_sum = scatter(big, BLOCK, s_big, gconv_ref)
    advance(conv_sum)
    for _ in range(4):
        advance(weights)

    def unpack(g, _):
        y_lo, zz = lax.div(g, 4), lax.rem(g, 4)
        for i in range(16):
            at = {"x": i % 4, "y": 2 * ((i // 4) % 2) + y_lo, "z": zz}
            for j, (a, b, c) in enumerate(ORDERS):
                block = bufs[j][i // 8, at[a], at[b], at[c]].astype(jnp.float32)
                wide[81 * i : 81 * i + 81, LANES * j : LANES * (j + 1)] = block[:81]
        full[pl.ds(pl.multiple_of(g * 1296, 16), 1296)] = wide[...].astype(jnp.bfloat16)
        return 0

    lax.fori_loop(0, 8, unpack, 0)
    advance(conv_sum)

    def back(k, acc):
        m = 26 - k
        rows = g_taps[lax.rem(m, 9), pl.ds(pl.multiple_of(16 * lax.div(m, 9), 16), PIXELS), :]
        kernel = full[pl.ds(pl.multiple_of(k * CHANS, CHANS), CHANS), :]
        return acc + dot(rows, kernel, (1, 1))

    def ahead_conv(k, acc):
        rows = a_taps[lax.rem(k, 9), pl.ds(pl.multiple_of(16 * lax.div(k, 9), 16), PIXELS), :]
        kernel = full[pl.ds(pl.multiple_of(k * CHANS, CHANS), CHANS), :]
        return acc + dot(rows, kernel)

    acc = lax.fori_loop(0, TAPS, back, jnp.zeros((PIXELS, CHANS), jnp.float32))
    xhat = act32[...]
    z = xhat * gain + shift
    sigma = 1.0 / (1.0 + jnp.exp(-z))
    pre = acc * (sigma * (1.0 + z * (1.0 - sigma)))
    wide_pre = gbuf.at[pl.ds(0, PIXELS)]
    wide_pre[...] = pre
    total2 = []
    sums2 = sum_steps(f, r, sum_rows(pre, pre * xhat), total2.append, row2, frame2, s_sum2)
    next(sums2)
    advance(conv_sum)
    next(sums2)
    acc = lax.fori_loop(0, TAPS, ahead_conv, jnp.zeros((PIXELS, CHANS), jnp.float32))
    code = acc + d_in[...].astype(jnp.float32).reshape(PIXELS, CHANS)
    code_ref[...] = code.reshape(16, 16, CHANS).astype(jnp.bfloat16)
    next(sums2, None)
    gshift_ref[...] = total2[0][0:1]
    ggain_ref[...] = total2[0][1:2]
    means = group_sum(total2[0] * gain, mask[...]) / TALLY
    grown = rstd * (wide_pre[...] * gain - means[0:1] - act32[...] * means[1:2]) + grad32[...]
    l_out[0:16] = grown.reshape(16, 16, CHANS).astype(jnp.bfloat16)
    l_out[16] = jnp.zeros((16, CHANS), jnp.bfloat16)
    l_in[f] = l_out[pl.ds(f, 2)]
    lat_ops = spread_start(f, r, l_out, l_in, 2, s_lat)
    waiting += lat_ops
    advance(conv_sum)
    for op in lat_ops:
        op.wait_recv()
    got = l_in[...].astype(jnp.float32)

    def by_rows(block):
        return jnp.concatenate([block[:, :8].reshape(128, CHANS), block[:, 8:].reshape(128, CHANS)],
                               0).astype(jnp.bfloat16)

    lat, after = by_rows(got[:, 0]), by_rows(got[:, 1])
    thin = gbuf.at[pl.ds(0, 3 * CHANS)]
    thin[0:CHANS, :] = only(f > 0, dot(before[...].reshape(PIXELS, CHANS), lat, (0, 0)))
    thin[CHANS : 2 * CHANS, :] = dot(video[0].reshape(PIXELS, CHANS), lat, (0, 0))
    thin[2 * CHANS :, :] = dot(video[1].reshape(PIXELS, CHANS), lat, (0, 0))
    pack_rows(thin, 0, 8, 0, 9, 16, [s[0] for s in small])
    down_sum = scatter(small, 16, s_small, gdown_ref)
    advance(down_sum)
    even = dot(lat, wd[CHANS : 2 * CHANS, :], (1, 1))
    odd = dot(lat, wd[2 * CHANS :, :], (1, 1)) + dot(after, wd[:CHANS, :], (1, 1))
    gvideo_ref[0] = even.reshape(2, 128, CHANS).astype(jnp.bfloat16)
    gvideo_ref[1] = odd.reshape(2, 128, CHANS).astype(jnp.bfloat16)
    interleave(conv_sum + down_sum)
    for op in waiting:
        op.wait_send()


def body(video, down_weight, conv_weight, norm_gain_vector, norm_shift_vector, output_gradient):
    lane = jnp.arange(CHANS) // 12
    mask = (lane[:, None] == lane[None, :]).astype(jnp.float32)
    vmem = pl.BlockSpec(memory_space=pltpu.VMEM)
    bf16, f32 = jnp.bfloat16, jnp.float32

    def sems(count):
        return [pltpu.SemaphoreType.DMA((count,)), pltpu.SemaphoreType.DMA((count,))]

    buf = pltpu.VMEM((2, 4, 4, 4, BLOCK, LANES), bf16)
    rows = pltpu.VMEM((384, CHANS), bf16)
    scratch = [buf] * 3 + scatter_scratch(BLOCK) * 3 + scatter_scratch(16) * 3 + [
        pltpu.VMEM((27 * CHANS, CHANS), bf16),
        pltpu.VMEM((8 * CHANS, CHANS), f32),
        pltpu.VMEM((1296, CHANS), f32),
        pltpu.VMEM((9, 288, CHANS), bf16),
        pltpu.VMEM((9, 288, CHANS), bf16),
        pltpu.VMEM((3, 512, LANES), f32),
        pltpu.VMEM((3, 64, LANES), f32),
        pltpu.VMEM((3, PIXELS, LANES), f32),
        rows, rows, rows, rows,
        pltpu.VMEM((2, 128, CHANS), bf16),
        pltpu.VMEM((16, 16, CHANS), bf16),
        pltpu.VMEM((16, 16, CHANS), bf16),
        pltpu.VMEM((17, 16, CHANS), bf16),
        pltpu.VMEM((16, 2, 16, CHANS), bf16),
        pltpu.VMEM((8, 8, CHANS), f32),
        pltpu.VMEM((16, 8, CHANS), f32),
        pltpu.VMEM((8, 8, CHANS), f32),
        pltpu.VMEM((16, 8, CHANS), f32),
        pltpu.VMEM((PIXELS, CHANS), f32),
        pltpu.VMEM((PIXELS, CHANS), f32),
    ]
    scratch += sems(48) + sems(48) + sems(48) + sems(22) + sems(22) + sems(15) + sems(15)
    scratch += sems(8) + sems(8) + sems(1)
    code, gvideo, gconv, gdown, ggain, gshift = pl.pallas_call(
        section_kernel,
        out_shape=(
            jax.ShapeDtypeStruct((16, 16, CHANS), bf16),
            jax.ShapeDtypeStruct((2, 2, 128, CHANS), bf16),
            jax.ShapeDtypeStruct((81, CHANS), f32),
            jax.ShapeDtypeStruct((9, CHANS), f32),
            jax.ShapeDtypeStruct((1, CHANS), f32),
            jax.ShapeDtypeStruct((1, CHANS), f32),
        ),
        in_specs=[vmem] * 7,
        out_specs=(vmem,) * 6,
        scratch_shapes=scratch,
        compiler_params=pltpu.CompilerParams(
            collective_id=0, has_side_effects=True, vmem_limit_bytes=63 * 2**20),
    )(video, down_weight, conv_weight, norm_gain_vector.reshape(1, CHANS),
      norm_shift_vector.reshape(1, CHANS), output_gradient.reshape(16, 16, CHANS), mask)
    return (code.reshape(16, 2, 8, CHANS), gvideo, gconv, gdown, ggain.reshape(CHANS),
            gshift.reshape(CHANS))


def solution(mesh):
    return jax.shard_map(
        body,
        mesh=mesh,
        in_specs=(
            P("frame", "row", None, None),
            P(),
            P(("frame", "row"), None),
            P(),
            P(),
            P(None, "row", "frame", None),
        ),
        out_specs=(
            P(None, "row", "frame", None),
            P("frame", "row", None, None),
            P(("frame", "row"), None),
            P(("frame", "row"), None),
            P(),
            P(),
        ),
        check_vma=False,
    )
```

time: 246 us -> 138 us (0.56); the launches traced: 242 us -> 138 us
  starting transfers between devices: 38.7 us -> 0 us
  local copies, waits for them, and re-layouts: 28.3 us -> 5.81 us
  matrix products: 21 us -> 0 us
  waiting for transfers between devices: 9.81 us -> 0 us
  Pallas kernels: 135 us -> 128 us
  other arithmetic: 7.07 us -> 3.53 us
    ppermute x10 -> x0, starting transfers between devices: 24.9 us -> none  [the longest x4 15.2 us: extended(): lax.ppermute(lax.slice_in_dim(block, block.shape[dim] - width, None, axis...]
    dot_general x8 -> x0, matrix products: 21 us -> none  [the longest x2 8.89 us: contract_rows(): lax.dot_general(left, right, (((0,), (0,)), ((), ())), preferred_element_...]
    all_to_all x2 -> x0, starting transfers between devices: 13.8 us -> none  [the longest x1 8.38 us: body(): lax.all_to_all(latent_gradient, 'frame', split_axis=0, concat_axis=2, til...]
    transpose x2 -> x0, local copies, waits for them, and re-layouts: 13.1 us -> none  [the longest x1 11.6 us: body(): kernel_full.reshape(27, chans, chans).transpose(0, 2, 1)]
    pallas_call x4 -> x1, Pallas kernels: 135 us -> 128 us  [body(): pl.pallas_call(section_kernel, out_shape=(jax.ShapeDtypeStruct((16, 16, C...]
    slice x9 -> x0, local copies, waits for them, and re-layouts: 6.84 us -> none  [the longest x2 2.92 us: body(): grad_conv, grad_down = (both[:81], both[81:90])]
    all_to_all x2 -> x0, waiting for transfers between devices: 6.64 us -> none  [the longest x1 6.64 us: body(): lax.all_to_all(down_frame, 'frame', split_axis=2, concat_axis=0, tiled=True)]
    concatenate x8 -> x0, other arithmetic: 4.26 us -> none  [the longest x6 2.92 us: extended(): block = jnp.concatenate([low, block, high], axis=dim)]
  transfers between devices with their start and end apart: 12 -> 0, of which waited for: 4 -> 0; matrix products, arithmetic and copies ran while one was open for 13% -> 0% of each run, Pallas kernels for 21% -> 0%
where the time goes in v2:
time: 138 us
  Pallas kernels  128 us (93%)
  local copies, waits for them, and re-layouts  5.81 us (4%)
  other arithmetic  3.53 us (3%)
    pallas_call x1, Pallas kernels, body(): pl.pallas_call(section_kernel, out_shape=(jax.ShapeDtypeStruct((16, 16, C...  128 us
    unnamed x12, local copies, waits for them, and re-layouts  4 us

profile of v2, /device:TPU:0, one launch (start us, length us, event | category | flops | bytes accessed | tf_op | source)
XLA Modules:
  0.0 137.5 jit_solution(17701629976337098623)
XLA Ops:
  0.6 0.0 copy-start.3
  0.6 1.3 reshape.56.gain_ref
  1.9 0.0 copy-done.3
  1.9 0.6 reshape.57.shift_ref
  2.5 0.9 compare_convert_fusion.mask
  3.4 127.5 %shard_map.109 = (bf16[16,16,384]{2,1,0:T(8,128)(2,1)}, bf16[2,2,128,384]{3,2,1,0:T(8,128)(2,1)}, f32[81,384]{1,0:T(8,128)}, f32[9,384]{1,0:T(8,128)}, f32[1,384]{1,0:T(1,128)}, /*index=5*/f32[1,384]{1,0:T(1,128)}) custom-call(bf16[2,2,128,384]{3,2,1,0:T(8,128)(2,1)} %video.1, bf16[1152,384]{1,0:T(8,128)(2,1)} %wd.1, bf16[81,384]{1,0:T(8,128)(2,1)} %w_ref.1, ...), custom_call_target="tpu_custom_call" | custom-call | tf_op jit(solution)/shard_map/pallas_call | solution.py:621
  131.0 0.0 copy-start
  131.0 1.3 reduce
  132.3 1.3 reduce.1
  133.6 1.6 %copy.16 = bf16[16,2,8,384]{3,2,1,0:T(8,128)(2,1)} copy(bf16[16,2,8,384]{3,2,1,0:T(8,128)(2,1)} %bitcast.2) | data formatting | bytes 393216
  135.2 0.0 copy-done
  135.2 0.0 copy-start.1
  135.2 0.7 copy.17
  135.9 0.3 copy-done.1
  136.2 0.0 copy-start.2
  136.2 0.7 copy.18
  136.9 0.1 copy-done.2
  136.9 0.6 copy.19
  (1 shorter events, 0.0 us)
Async XLA Ops:
  0.6 1.3 copy-start.3
  131.0 4.2 %copy-start = (bf16[2,2,128,384]{3,2,1,0:T(8,128)(2,1)S(1)}, bf16[2,2,128,384]{3,2,1,0:T(8,128)(2,1)}, u32[]{:S(2)}) copy-start(bf16[2,2,128,384]{3,2,1,0:T(8,128)(2,1)} %get-tuple-element.25) | copy-start | bytes 1179652
  135.2 1.0 copy-start.1
  136.2 0.7 copy-start.2

commit v3 on v2

--- a/solution.py
+++ b/solution.py
@@ -41,7 +41,7 @@
     barrier = pltpu.get_barrier_semaphore()
     for device in devices:
         pl.semaphore_signal(barrier, inc=1, device_id=device, device_id_type=MESH)
-    pl.semaphore_wait(barrier, len(devices))
+    return lambda: pl.semaphore_wait(barrier, len(devices))
 
 
 def remote(src, dst, sems, index, device):
@@ -69,19 +69,21 @@
         sent.append(op)
         return op
 
+    mine = buf.at[core, ca, cb, cc]
+    near = [start(mine, mine, device_at(shifted(pos, c, s), core)) for s in (1, -1, 2)]
+    yield
+    for op in near:
+        op.wait_recv()
     whole = {
-        c: lambda i: buf.at[core, ca, cb, i],
         b: lambda i: buf.at[core, ca, i],
         a: lambda i: buf.at[core, i],
     }
-    half = BLOCK // 2
     parts = {
-        c: lambda i, h: buf.at[core, ca, cb, i, pl.ds(h * half, half)],
         b: lambda i, h: buf.at[core, ca, i, pl.ds(2 * h, 2)],
         a: lambda i, h: buf.at[core, i, pl.ds(2 * h, 2)],
     }
     other = device_at(pos, 1 - core)
-    for axis in (c, b, a):
+    for axis in (b, a):
         me = pos[axis]
         up, down = shifted(pos, axis, 1), shifted(pos, axis, -1)
         mine, one, ref = whole[axis](me), whole[axis], parts[axis]
@@ -105,7 +107,7 @@
     start(buf.at[core, far], buf.at[core, far], other)
     yield
     for k, op in enumerate(sent):
-        if k in (10, 12, 14, 15):
+        if k in (9, 11, 13, 14):
             op.wait_recv()
         op.wait_send()
 
@@ -140,7 +142,6 @@
 def scatter_steps(pos, core, order, rows, piles, got, near, q, near_q, u, near_u, sems, base, out):
     a, b, c = order
     ca, cb, cc = pos[a], pos[b], pos[c]
-    half = rows // 2
     sent = []
 
     def start(src, dst, device):
@@ -193,31 +194,26 @@
         q[k] = total
 
     add_into(4, put_q, pair(ca) + [lambda k: near_c[k], lambda k: near_d[k]])
-    for axis, v, near_v, low, high, lower, upper in (
-        (b, q, near_q, lambda i: q.at[i, pl.ds(0, 2)], lambda i: q.at[i, pl.ds(2, 2)],
-         pl.ds(0, 2), pl.ds(2, 2)),
-        (c, u, near_u, lambda i: u.at[i, pl.ds(0, half)], lambda i: u.at[i, pl.ds(half, half)],
-         pl.ds(0, half), pl.ds(half, half)),
-    ):
-        far, up, down, me = at(axis, 2), at(axis, 1), at(axis, -1), pos[axis]
-        near_a, near_b, near_c, near_d = near_v
-        op_a = start(low(far), near_a, toward(axis, 1))
-        op_b = start(high(far), near_b, toward(axis, -1))
-        yield
-        op_a.wait_recv()
-        v[up, lower] = v[up, lower] + near_a[...]
-        op_c = start(v.at[up], near_c, toward(axis, 1))
-        op_b.wait_recv()
-        v[down, upper] = v[down, upper] + near_b[...]
-        op_d = start(v.at[down], near_d, toward(axis, -1))
-        yield
-        op_c.wait_recv()
-        op_d.wait_recv()
-        total = v[me] + near_c[...] + near_d[...]
-        if axis == b:
-            u[...] = total
-        else:
-            out(total)
+    far, up, down = at(b, 2), at(b, 1), at(b, -1)
+    near_a, near_b, near_c, near_d = near_q
+    op_a = start(q.at[far, pl.ds(0, 2)], near_a, toward(b, 1))
+    op_b = start(q.at[far, pl.ds(2, 2)], near_b, toward(b, -1))
+    yield
+    op_a.wait_recv()
+    q[up, pl.ds(0, 2)] = q[up, pl.ds(0, 2)] + near_a[...]
+    op_c = start(q.at[up], near_c, toward(b, 1))
+    op_b.wait_recv()
+    q[down, pl.ds(2, 2)] = q[down, pl.ds(2, 2)] + near_b[...]
+    op_d = start(q.at[down], near_d, toward(b, -1))
+    yield
+    op_c.wait_recv()
+    op_d.wait_recv()
+    u[...] = q[cb] + near_c[...] + near_d[...]
+    ops = [start(u.at[at(c, s)], near_u.at[n], toward(c, s)) for n, s in enumerate((1, -1, 2))]
+    yield
+    for op in ops:
+        op.wait_recv()
+    out(u[cc] + near_u[0] + near_u[1] + near_u[2])
     yield
     for op in sent:
         op.wait_send()
@@ -230,10 +226,67 @@
     def f32(*lead):
         return pltpu.VMEM(lead + (rows, LANES), jnp.float32)
 
-    half = pltpu.VMEM((rows // 2, LANES), jnp.float32)
     one = [bf(2, 4, 4, 4), bf(4, 4, 4), bf(2, 4), bf(2, 4), bf(4, 4), bf(4, 4), f32(4, 4),
-           f32(2), f32(2), f32(4), f32(4), f32(4), half, half, f32(), f32()]
+           f32(2), f32(2), f32(4), f32(4), f32(4), f32(3)]
     return one
+
+
+def direct_scratch(rows):
+    def bf(*lead):
+        return pltpu.VMEM(lead + (rows, LANES), jnp.bfloat16)
+
+    def f32(*lead):
+        return pltpu.VMEM(lead + (rows, LANES), jnp.float32)
+
+    return [bf(2, 4, 4, 4), bf(4, 4, 4), bf(3, 4, 4), f32(4, 4), f32(3, 4), f32(4), f32(3)]
+
+
+def direct_steps(pos, core, order, piles, got, near_p, q, near_q, u, near_u, sems, base, out):
+    a, b, c = order
+    ca = pos[a]
+    sent = []
+
+    def start(src, dst, device):
+        op = remote(src, dst, sems, base + len(sent), device)
+        op.start()
+        sent.append(op)
+        return op
+
+    def exchange(axis, ref, near):
+        return [start(ref.at[shifted(pos, axis, s)[axis]], near.at[n],
+                      device_at(shifted(pos, axis, s), core)) for n, s in enumerate((1, -1, 2))]
+
+    swap = start(piles.at[1 - core], got, device_at(pos, 1 - core))
+    yield
+    swap.wait_recv()
+    for s in (2, 1, -1):
+        i = shifted(pos, a, s)[a]
+        total = piles[core, i].astype(jnp.float32) + got[i].astype(jnp.float32)
+        piles[core, i] = total.astype(jnp.bfloat16)
+    ops = exchange(a, piles.at[core], near_p)
+    yield
+    total = piles[core, ca].astype(jnp.float32) + got[ca].astype(jnp.float32)
+    for n, op in enumerate(ops):
+        op.wait_recv()
+        total = total + near_p[n].astype(jnp.float32)
+    q[...] = total
+    ops = exchange(b, q, near_q)
+    yield
+    total = q[pos[b]]
+    for n, op in enumerate(ops):
+        op.wait_recv()
+        total = total + near_q[n]
+    u[...] = total
+    ops = exchange(c, u, near_u)
+    yield
+    total = u[pos[c]]
+    for n, op in enumerate(ops):
+        op.wait_recv()
+        total = total + near_u[n]
+    out(total)
+    yield
+    for op in sent:
+        op.wait_send()
 
 
 def sum_steps(f, r, x, done, row_in, frame_in, sems):
@@ -388,7 +441,7 @@
     lax.fori_loop(0, groups, pack, 0)
 
 
-def section_kernel(video, wd, w_ref, gain_ref, shift_ref, og_ref, mask,
+def section_kernel(video, wd, w_ref, gain_ref, shift_ref, og_ref,
                    code_ref, gvideo_ref, gconv_ref, gdown_ref, ggain_ref, gshift_ref, *scratch):
     refs = list(scratch)
 
@@ -398,10 +451,10 @@
         return out
 
     bufs = take(3)
-    big = [take(16) for _ in range(3)]
-    small = [take(16) for _ in range(3)]
+    big = [take(13) for _ in range(3)]
+    small = [take(7) for _ in range(3)]
     (full, gbuf, wide, a_taps, g_taps, ext, side, lanes, h_out, h_in, g_out, g_in, before,
-     d_out, d_in, l_out, l_in, row1, frame1, row2, frame2, act32, grad32) = take(23)
+     d_out, d_in, l_out, l_in, row1, frame1, row2, frame2, act32, grad32, mask) = take(24)
     sem = [(refs[2 * i], refs[2 * i + 1]) for i in range(len(refs) // 2)]
     s_gather, s_big, s_small, s_sum1, s_sum2, s_down, s_lat, s_act, s_grad, s_video = sem
 
@@ -410,32 +463,37 @@
     peers += [(lax.rem(f + s, 16), r) for s in range(1, 16)]
     peers += [device_at(shifted(pos, "y", s), core) for s in (1, -1)]
     peers += [(lax.rem(f + s, 16), lax.rem(r + t, 8)) for s in (1, 15) for t in (1, 7)]
-    greet(peers)
+    arrived = greet(peers)
     waiting = []
+
+    def advance(steps):
+        for step in steps:
+            next(step, None)
 
     for j, (a, b, c) in enumerate(ORDERS):
         block = w_ref[:, LANES * j : LANES * (j + 1)].astype(jnp.float32)
         block = jnp.concatenate([block, jnp.zeros((BLOCK - 81, LANES), jnp.float32)], 0)
         bufs[j][core, pos[a], pos[b], pos[c]] = block.astype(jnp.bfloat16)
-    weights = [gather_steps(pos, core, order, bufs[j], s_gather, j * GATHER_COPIES)
-               for j, order in enumerate(ORDERS)]
-
-    def advance(steps):
-        for step in steps:
-            next(step, None)
+    grad32[...] = og_ref[...].astype(jnp.float32).reshape(PIXELS, CHANS)
+    group = [jnp.floor((lax.broadcasted_iota(jnp.int32, (CHANS, CHANS), d).astype(jnp.float32) + 0.5)
+                       / 12.0) for d in range(2)]
+    mask[...] = jnp.where(group[0] == group[1], 1.0, 0.0)
+    v0 = video[0].reshape(PIXELS, CHANS)
+    v1 = video[1].reshape(PIXELS, CHANS)
+    act32[...] = dot(v0, wd[CHANS : 2 * CHANS, :]) + dot(v1, wd[2 * CHANS :, :])
+    arrived()
 
     ahead = remote(video.at[1], before, s_video, 0, (lax.rem(f + 1, 16), r))
     ahead.start()
     waiting.append(ahead)
+    weights = [gather_steps(pos, core, order, bufs[j], s_gather, j * GATHER_COPIES)
+               for j, order in enumerate(ORDERS)]
     advance(weights)
-    grad32[...] = og_ref[...].astype(jnp.float32).reshape(PIXELS, CHANS)
     grad_ops = halo_start(f, r, grad32, lanes, g_out, g_in, s_grad)
     waiting += grad_ops
-
-    v0 = video[0].reshape(PIXELS, CHANS)
-    v1 = video[1].reshape(PIXELS, CHANS)
-    down = dot(v0, wd[CHANS : 2 * CHANS, :]) + dot(v1, wd[2 * CHANS :, :])
+    advance(weights)
     ahead.wait_recv()
+    down = act32[...]
     vb = before[...].reshape(PIXELS, CHANS)
     down = down + only(f > 0, dot(vb, wd[:CHANS, :]))
     down = down.reshape(2, 16, 8, CHANS)
@@ -443,27 +501,27 @@
     d_in[f] = d_out[f]
     down_ops = spread_start(f, r, d_out, d_in, 1, s_down)
     waiting += down_ops
-    advance(weights)
-    halo_finish(f, r, grad_ops, grad32, g_in, ext, side, g_taps, 0)
-    for op in down_ops:
-        op.wait_recv()
-    latent = d_in[...].astype(jnp.float32).reshape(PIXELS, CHANS)
 
     def sum_rows(first, second):
         return jnp.concatenate([jnp.sum(first, 0, keepdims=True), jnp.sum(second, 0, keepdims=True),
                                 jnp.zeros((6, CHANS), jnp.float32)], 0)
 
+    mine = d_out[...].astype(jnp.float32).reshape(PIXELS, CHANS)
     total = []
-    sums = sum_steps(f, r, sum_rows(latent, latent * latent), total.append, row1, frame1, s_sum1)
+    sums = sum_steps(f, r, sum_rows(mine, mine * mine), total.append, row1, frame1, s_sum1)
     next(sums)
     advance(weights)
     next(sums)
+    halo_finish(f, r, grad_ops, grad32, g_in, ext, side, g_taps, 0)
     advance(weights)
+    for op in down_ops:
+        op.wait_recv()
+    latent = d_in[...].astype(jnp.float32).reshape(PIXELS, CHANS)
     next(sums, None)
     moments = group_sum(total[0], mask[...]) / TALLY
     mean = moments[0:1]
     rstd = lax.rsqrt(moments[1:2] - mean * mean + 1e-06)
-    gain, shift = gain_ref[...], shift_ref[...]
+    gain, shift = gain_ref[...].reshape(1, CHANS), shift_ref[...].reshape(1, CHANS)
     act32[...] = (latent - mean) * rstd
     xhat = act32[...]
     z = xhat * gain + shift
@@ -488,8 +546,6 @@
 
         lax.fori_loop(0, high - low, tap, 0)
         pack_rows(gbuf, 2592 * part - CHANS * low, 2, 2 * part, 81, BLOCK, piles)
-        if part == 1:
-            advance(weights)
 
     def scatter(sets, rows, sems, out_ref):
         def run(j, order):
@@ -498,14 +554,16 @@
             def out(total):
                 out_ref[:, LANES * j : LANES * (j + 1)] = total[: out_ref.shape[0]]
 
+            if rows == 16:
+                return direct_steps(pos, core, order, *s, sems, j * SCATTER_COPIES, out)
             return scatter_steps(pos, core, order, rows, s[0], s[1], s[2:6], s[6], s[7:11],
-                                 s[11], s[12:16], sems, j * SCATTER_COPIES, out)
+                                 s[11], s[12], sems, j * SCATTER_COPIES, out)
 
         return [run(j, order) for j, order in enumerate(ORDERS)]
 
     conv_sum = scatter(big, BLOCK, s_big, gconv_ref)
     advance(conv_sum)
-    for _ in range(4):
+    for _ in range(3):
         advance(weights)
 
     def unpack(g, _):
@@ -521,18 +579,25 @@
     lax.fori_loop(0, 8, unpack, 0)
     advance(conv_sum)
 
-    def back(k, acc):
-        m = 26 - k
-        rows = g_taps[lax.rem(m, 9), pl.ds(pl.multiple_of(16 * lax.div(m, 9), 16), PIXELS), :]
-        kernel = full[pl.ds(pl.multiple_of(k * CHANS, CHANS), CHANS), :]
-        return acc + dot(rows, kernel, (1, 1))
-
-    def ahead_conv(k, acc):
-        rows = a_taps[lax.rem(k, 9), pl.ds(pl.multiple_of(16 * lax.div(k, 9), 16), PIXELS), :]
-        kernel = full[pl.ds(pl.multiple_of(k * CHANS, CHANS), CHANS), :]
-        return acc + dot(rows, kernel)
-
-    acc = lax.fori_loop(0, TAPS, back, jnp.zeros((PIXELS, CHANS), jnp.float32))
+    def back(n, acc):
+        rows, kernels = [], []
+        for e in range(3):
+            k = 3 * n + e
+            m = 26 - k
+            rows.append(g_taps[lax.rem(m, 9), pl.ds(pl.multiple_of(16 * lax.div(m, 9), 16), PIXELS), :])
+            kernels.append(full[pl.ds(pl.multiple_of(k * CHANS, CHANS), CHANS), :])
+        return acc + dot(jnp.concatenate(rows, 1), jnp.concatenate(kernels, 1), (1, 1))
+
+    def ahead_conv(n, acc):
+        rows = []
+        for e in range(3):
+            k = 3 * n + e
+            rows.append(a_taps[lax.rem(k, 9), pl.ds(pl.multiple_of(16 * lax.div(k, 9), 16), PIXELS), :])
+        kernel = full[pl.ds(pl.multiple_of(n * 3 * CHANS, CHANS), 3 * CHANS), :]
+        return acc + dot(jnp.concatenate(rows, 1), kernel)
+
+    acc = jnp.zeros((PIXELS, CHANS), jnp.float32)
+    acc = lax.fori_loop(0, 9, back, acc)
     xhat = act32[...]
     z = xhat * gain + shift
     sigma = 1.0 / (1.0 + jnp.exp(-z))
@@ -543,13 +608,14 @@
     sums2 = sum_steps(f, r, sum_rows(pre, pre * xhat), total2.append, row2, frame2, s_sum2)
     next(sums2)
     advance(conv_sum)
+    acc = lax.fori_loop(0, 3, ahead_conv, jnp.zeros((PIXELS, CHANS), jnp.float32))
     next(sums2)
-    acc = lax.fori_loop(0, TAPS, ahead_conv, jnp.zeros((PIXELS, CHANS), jnp.float32))
+    acc = lax.fori_loop(3, 9, ahead_conv, acc)
     code = acc + d_in[...].astype(jnp.float32).reshape(PIXELS, CHANS)
     code_ref[...] = code.reshape(16, 16, CHANS).astype(jnp.bfloat16)
     next(sums2, None)
-    gshift_ref[...] = total2[0][0:1]
-    ggain_ref[...] = total2[0][1:2]
+    gshift_ref[...] = total2[0][0:1].reshape(CHANS)
+    ggain_ref[...] = total2[0][1:2].reshape(CHANS)
     means = group_sum(total2[0] * gain, mask[...]) / TALLY
     grown = rstd * (wide_pre[...] * gain - means[0:1] - act32[...] * means[1:2]) + grad32[...]
     l_out[0:16] = grown.reshape(16, 16, CHANS).astype(jnp.bfloat16)
@@ -578,14 +644,22 @@
     odd = dot(lat, wd[2 * CHANS :, :], (1, 1)) + dot(after, wd[:CHANS, :], (1, 1))
     gvideo_ref[0] = even.reshape(2, 128, CHANS).astype(jnp.bfloat16)
     gvideo_ref[1] = odd.reshape(2, 128, CHANS).astype(jnp.bfloat16)
-    interleave(conv_sum + down_sum)
+    advance(down_sum)
+    advance(conv_sum)
+    advance(down_sum)
+    advance(down_sum)
+    advance(conv_sum)
+    interleave(down_sum + conv_sum)
     for op in waiting:
         op.wait_send()
 
 
+def hand_out(*refs):
+    for source, target in zip(refs[:6], refs[6:]):
+        target[...] = source[...]
+
+
 def body(video, down_weight, conv_weight, norm_gain_vector, norm_shift_vector, output_gradient):
-    lane = jnp.arange(CHANS) // 12
-    mask = (lane[:, None] == lane[None, :]).astype(jnp.float32)
     vmem = pl.BlockSpec(memory_space=pltpu.VMEM)
     bf16, f32 = jnp.bfloat16, jnp.float32
 
@@ -594,7 +668,7 @@
 
     buf = pltpu.VMEM((2, 4, 4, 4, BLOCK, LANES), bf16)
     rows = pltpu.VMEM((384, CHANS), bf16)
-    scratch = [buf] * 3 + scatter_scratch(BLOCK) * 3 + scatter_scratch(16) * 3 + [
+    scratch = [buf] * 3 + scatter_scratch(BLOCK) * 3 + direct_scratch(16) * 3 + [
         pltpu.VMEM((27 * CHANS, CHANS), bf16),
         pltpu.VMEM((8 * CHANS, CHANS), f32),
         pltpu.VMEM((1296, CHANS), f32),
@@ -615,28 +689,34 @@
         pltpu.VMEM((16, 8, CHANS), f32),
         pltpu.VMEM((PIXELS, CHANS), f32),
         pltpu.VMEM((PIXELS, CHANS), f32),
+        pltpu.VMEM((CHANS, CHANS), f32),
     ]
     scratch += sems(48) + sems(48) + sems(48) + sems(22) + sems(22) + sems(15) + sems(15)
     scratch += sems(8) + sems(8) + sems(1)
-    code, gvideo, gconv, gdown, ggain, gshift = pl.pallas_call(
+    results = pl.pallas_call(
         section_kernel,
         out_shape=(
             jax.ShapeDtypeStruct((16, 16, CHANS), bf16),
             jax.ShapeDtypeStruct((2, 2, 128, CHANS), bf16),
             jax.ShapeDtypeStruct((81, CHANS), f32),
             jax.ShapeDtypeStruct((9, CHANS), f32),
-            jax.ShapeDtypeStruct((1, CHANS), f32),
-            jax.ShapeDtypeStruct((1, CHANS), f32),
+            jax.ShapeDtypeStruct((CHANS,), f32),
+            jax.ShapeDtypeStruct((CHANS,), f32),
         ),
-        in_specs=[vmem] * 7,
+        in_specs=[vmem] * 6,
         out_specs=(vmem,) * 6,
         scratch_shapes=scratch,
         compiler_params=pltpu.CompilerParams(
             collective_id=0, has_side_effects=True, vmem_limit_bytes=63 * 2**20),
-    )(video, down_weight, conv_weight, norm_gain_vector.reshape(1, CHANS),
-      norm_shift_vector.reshape(1, CHANS), output_gradient.reshape(16, 16, CHANS), mask)
-    return (code.reshape(16, 2, 8, CHANS), gvideo, gconv, gdown, ggain.reshape(CHANS),
-            gshift.reshape(CHANS))
+    )(video, down_weight, conv_weight, norm_gain_vector, norm_shift_vector,
+      output_gradient.reshape(16, 16, CHANS))
+    code, gvideo, gconv, gdown, ggain, gshift = pl.pallas_call(
+        hand_out,
+        out_shape=tuple(jax.ShapeDtypeStruct(x.shape, x.dtype) for x in results),
+        in_specs=[vmem] * 6,
+        out_specs=(vmem,) * 6,
+    )(*results)
+    return (code.reshape(16, 2, 8, CHANS), gvideo, gconv, gdown, ggain, gshift)
 
 
 def solution(mesh):

time: 138 us -> 119 us (0.86)
  Pallas kernels: 128 us -> 118 us
  local copies, waits for them, and re-layouts: 5.81 us -> 0 us
  other arithmetic: 3.53 us -> 0 us
    pallas_call x1, Pallas kernels: 128 us -> 116 us  [body(): pl.pallas_call(section_kernel, out_shape=(jax.ShapeDtypeStruct((16, 16, C...]
    unnamed x12 -> x0, local copies, waits for them, and re-layouts: 4 us -> none
    pallas_call x2 -> x0, other arithmetic: 2.59 us -> none  [body(): pl.pallas_call(section_kernel, out_shape=(jax.ShapeDtypeStruct((16, 16, C...]
    pallas_call x0 -> x1, Pallas kernels: none -> 2.04 us  [body(): pl.pallas_call(hand_out, out_shape=tuple((jax.ShapeDtypeStruct(x.shape, x...]
    reshape x2 -> x0, local copies, waits for them, and re-layouts: 1.81 us -> none  [the longest x1 1.25 us: body(): norm_gain_vector.reshape(1, CHANS)]
where the time goes in v3:
time: 119 us; the launch traced here: 118 us
  Pallas kernels  118 us (99%)
    pallas_call x1, Pallas kernels, body(): pl.pallas_call(section_kernel, out_shape=(jax.ShapeDtypeStruct((16, 16, C...  116 us

profile of v3, /device:TPU:0, one launch (start us, length us, event | category | flops | bytes accessed | tf_op | source)
XLA Modules:
  0.0 118.3 jit_solution(11113815959592313112)
XLA Ops:
  0.6 115.6 %shard_map.109 = (bf16[16,16,384]{2,1,0:T(8,128)(2,1)}, bf16[2,2,128,384]{3,2,1,0:T(8,128)(2,1)}, f32[81,384]{1,0:T(8,128)}, f32[9,384]{1,0:T(8,128)}, f32[384]{0:T(512)}, /*index=5*/f32[384]{0:T(512)}) custom-call(bf16[2,2,128,384]{3,2,1,0:T(8,128)(2,1)} %video.1, bf16[1152,384]{1,0:T(8,128)(2,1)} %wd.1, bf16[81,384]{1,0:T(8,128)(2,1)} %w_ref.1, ...), custom_call_target="tpu_custom_call" | custom-call | tf_op jit(solution)/shard_map/pallas_call | solution.py:696
  116.3 2.0 %shard_map.110 = (bf16[16,16,384]{2,1,0:T(8,128)(2,1)}, bf16[2,2,128,384]{3,2,1,0:T(8,128)(2,1)}, f32[81,384]{1,0:T(8,128)}, f32[9,384]{1,0:T(8,128)}, f32[384]{0:T(512)}, /*index=5*/f32[384]{0:T(512)}) custom-call(bf16[16,16,384]{2,1,0:T(8,128)(2,1)} %get-tuple-element.18.refs_0_, bf16[2,2,128,384]{3,2,1,0:T(8,128)(2,1)} %get-tuple-element.19.refs_1_, ...), custom_call_target="tpu_custom_call" | custom-call | tf_op jit(solution)/shard_map/pallas_call | solution.py:713

commit v4 on v3

--- a/solution.py
+++ b/solution.py
@@ -55,7 +55,7 @@
     )
 
 
-GATHER_COPIES = 16
+GATHER_COPIES = 20
 
 
 def gather_steps(pos, core, order, buf, sems, base):
@@ -83,32 +83,37 @@
         a: lambda i, h: buf.at[core, i, pl.ds(2 * h, 2)],
     }
     other = device_at(pos, 1 - core)
+    swaps = []
     for axis in (b, a):
         me = pos[axis]
         up, down = shifted(pos, axis, 1), shifted(pos, axis, -1)
-        mine, one, ref = whole[axis](me), whole[axis], parts[axis]
-        first = start(mine, mine, device_at(up, core))
-        second = start(mine, mine, device_at(down, core))
+        one, part = whole[axis], parts[axis]
+        first = [start(part(me, h), part(me, h), device_at(up, core)) for h in (0,)]
+        second = [start(part(me, h), part(me, h), device_at(down, core)) for h in (1,)]
+        first += [start(part(me, h), part(me, h), device_at(up, core)) for h in (1,)]
+        second += [start(part(me, h), part(me, h), device_at(down, core)) for h in (0,)]
         if axis == a:
-            start(mine, mine, other)
+            swaps.append(start(one(me), one(me), other))
         yield
-        first.wait_recv()
-        third = start(ref(down[axis], 0), ref(down[axis], 0), device_at(up, core))
+        first[0].wait_recv()
+        third = start(part(down[axis], 0), part(down[axis], 0), device_at(up, core))
+        second[0].wait_recv()
+        fourth = start(part(up[axis], 1), part(up[axis], 1), device_at(down, core))
+        yield
+        first[1].wait_recv()
+        second[1].wait_recv()
         if axis == a:
-            start(one(down[axis]), one(down[axis]), other)
-        second.wait_recv()
-        fourth = start(ref(up[axis], 1), ref(up[axis], 1), device_at(down, core))
-        if axis == a:
-            start(one(up[axis]), one(up[axis]), other)
-        yield
+            swaps.append(start(one(down[axis]), one(down[axis]), other))
+            swaps.append(start(one(up[axis]), one(up[axis]), other))
+            yield
         third.wait_recv()
         fourth.wait_recv()
     far = shifted(pos, a, 2)[a]
-    start(buf.at[core, far], buf.at[core, far], other)
-    yield
-    for k, op in enumerate(sent):
-        if k in (9, 11, 13, 14):
-            op.wait_recv()
+    swaps.append(start(buf.at[core, far], buf.at[core, far], other))
+    yield
+    for op in swaps:
+        op.wait_recv()
+    for op in sent:
         op.wait_send()
 
 
@@ -125,7 +130,7 @@
         steps = left
 
 
-SCATTER_COPIES = 16
+SCATTER_COPIES = 20
 
 
 def add_into(count, target, terms):
@@ -139,7 +144,7 @@
     lax.fori_loop(0, count, step, 0)
 
 
-def scatter_steps(pos, core, order, rows, piles, got, near, q, near_q, u, near_u, sems, base, out):
+def scatter_steps(pos, core, order, rows, piles, got, near, q, q_out, near_q, u, near_u, sems, base, out):
     a, b, c = order
     ca, cb, cc = pos[a], pos[b], pos[c]
     sent = []
@@ -170,25 +175,29 @@
         return [lambda k: piles[core, i, k + first], lambda k: got[i, k + first]]
 
     near_a, near_b, near_c, near_d = near
+    low, high = pl.ds(0, 2), pl.ds(2, 2)
     swaps[0].wait_recv()
     add_into(4, store(far), pair(far))
-    op_a = start(piles.at[core, far, pl.ds(0, 2)], near_a, toward(a, 1))
-    op_b = start(piles.at[core, far, pl.ds(2, 2)], near_b, toward(a, -1))
+    op_a = start(piles.at[core, far, low], near_a, toward(a, 1))
+    op_b = start(piles.at[core, far, high], near_b, toward(a, -1))
     yield
     swaps[1].wait_recv()
+    add_into(2, lambda k, total: store(up)(k + 2, total), pair(up, 2))
+    late = [start(piles.at[core, up, high], near_c.at[high], toward(a, 1))]
+    swaps[2].wait_recv()
+    add_into(2, store(down), pair(down))
+    late.append(start(piles.at[core, down, low], near_d.at[low], toward(a, -1)))
+    yield
     op_a.wait_recv()
     add_into(2, store(up), pair(up) + [lambda k: near_a[k]])
-    add_into(2, lambda k, total: store(up)(k + 2, total), pair(up, 2))
-    op_c = start(piles.at[core, up], near_c, toward(a, 1))
-    swaps[2].wait_recv()
+    late.append(start(piles.at[core, up, low], near_c.at[low], toward(a, 1)))
     op_b.wait_recv()
-    add_into(2, store(down), pair(down))
     add_into(2, lambda k, total: store(down)(k + 2, total), pair(down, 2) + [lambda k: near_b[k]])
-    op_d = start(piles.at[core, down], near_d, toward(a, -1))
+    late.append(start(piles.at[core, down, high], near_d.at[high], toward(a, -1)))
     yield
     swaps[3].wait_recv()
-    op_c.wait_recv()
-    op_d.wait_recv()
+    for op in late:
+        op.wait_recv()
 
     def put_q(k, total):
         q[k] = total
@@ -196,19 +205,24 @@
     add_into(4, put_q, pair(ca) + [lambda k: near_c[k], lambda k: near_d[k]])
     far, up, down = at(b, 2), at(b, 1), at(b, -1)
     near_a, near_b, near_c, near_d = near_q
-    op_a = start(q.at[far, pl.ds(0, 2)], near_a, toward(b, 1))
-    op_b = start(q.at[far, pl.ds(2, 2)], near_b, toward(b, -1))
+    f32, bf16 = jnp.float32, jnp.bfloat16
+    for s, i in ((2, far), (1, up), (3, down)):
+        q_out[s] = q[i].astype(bf16)
+    op_a = start(q_out.at[2, low], near_a, toward(b, 1))
+    op_b = start(q_out.at[2, high], near_b, toward(b, -1))
+    late = [start(q_out.at[1, high], near_c.at[high], toward(b, 1)),
+            start(q_out.at[3, low], near_d.at[low], toward(b, -1))]
     yield
     op_a.wait_recv()
-    q[up, pl.ds(0, 2)] = q[up, pl.ds(0, 2)] + near_a[...]
-    op_c = start(q.at[up], near_c, toward(b, 1))
+    q_out[1, low] = (q[up, low] + near_a[...].astype(f32)).astype(bf16)
+    late.append(start(q_out.at[1, low], near_c.at[low], toward(b, 1)))
     op_b.wait_recv()
-    q[down, pl.ds(2, 2)] = q[down, pl.ds(2, 2)] + near_b[...]
-    op_d = start(q.at[down], near_d, toward(b, -1))
-    yield
-    op_c.wait_recv()
-    op_d.wait_recv()
-    u[...] = q[cb] + near_c[...] + near_d[...]
+    q_out[3, high] = (q[down, high] + near_b[...].astype(f32)).astype(bf16)
+    late.append(start(q_out.at[3, high], near_d.at[high], toward(b, -1)))
+    yield
+    for op in late:
+        op.wait_recv()
+    u[...] = q[cb] + near_c[...].astype(f32) + near_d[...].astype(f32)
     ops = [start(u.at[at(c, s)], near_u.at[n], toward(c, s)) for n, s in enumerate((1, -1, 2))]
     yield
     for op in ops:
@@ -227,7 +241,7 @@
         return pltpu.VMEM(lead + (rows, LANES), jnp.float32)
 
     one = [bf(2, 4, 4, 4), bf(4, 4, 4), bf(2, 4), bf(2, 4), bf(4, 4), bf(4, 4), f32(4, 4),
-           f32(2), f32(2), f32(4), f32(4), f32(4), f32(3)]
+           bf(4, 4), bf(2), bf(2), bf(4), bf(4), f32(4), f32(3)]
     return one
 
 
@@ -374,15 +388,36 @@
     return ops
 
 
-def halo_finish(f, r, ops, wide, into, ext, side, taps, first):
+def turn(block, e):
+    if e == 1:
+        return block
+    rows = block.reshape(-1, 8, CHANS)
+    return pltpu.roll(rows, 1 if e == 0 else 7, 1).reshape(block.shape)
+
+
+def put_rows(ext, e, first, value):
+    for j in range(3):
+        for t in range(16):
+            low = 32 * t + first
+            ext[3 * e + j, low : low + value.shape[1], :] = value[t, :, LANES * j : LANES * (j + 1)]
+
+
+def halo_fill(wide, ext, taps, first):
+    middle = wide[...].reshape(16, 2, 8, CHANS)
+    for e in range(3):
+        put_rows(ext, e, 8, turn(middle, e).reshape(16, 16, CHANS))
+    zeros = jnp.zeros((32, CHANS), jnp.bfloat16)
+    for i in range(9):
+        taps[i, pl.ds(0 if first else 256, 32), :] = zeros
+
+
+def halo_finish(f, r, ops, into, ext, side, taps, first):
     for op in ops:
         op.wait_recv()
     top, bottom, left, right = r > 0, r < 7, f > 0, f < 15
     edge = into[...].astype(jnp.float32)
-    middle = wide[...].reshape(16, 2, 8, CHANS)
-    above = only(top, edge[0:128]).reshape(16, 1, 8, CHANS)
-    below = only(bottom, edge[128:256]).reshape(16, 1, 8, CHANS)
-    base = jnp.concatenate([above, middle, below], 1)
+    above = only(top, edge[0:128]).reshape(16, 8, CHANS)
+    below = only(bottom, edge[128:256]).reshape(16, 8, CHANS)
     store_rows(side, 0, 64, 1, jnp.concatenate(
         [only(left, edge[256:288]), only(right, edge[288:320])], 0))
     corner = {
@@ -392,25 +427,21 @@
         (3, 2): only(bottom & right, edge[368:384]),
     }
     for e in range(3):
-        if e == 1:
-            store_rows(ext, 0, 512, 1, base.reshape(512, CHANS))
-        else:
-            turned = pltpu.roll(base.reshape(64, 8, CHANS), 1 if e == 0 else 7, 1)
-            store_rows(ext, 0, 512, 1, turned.reshape(512, CHANS))
+        put_rows(ext, e, 0, turn(above, e))
+        put_rows(ext, e, 24, turn(below, e))
+        shift = ext.at[pl.ds(3 * e, 3)]
+        if e != 1:
             col = 0 if e == 0 else 7
             for i in range(4):
                 if i in (0, 3):
                     value = corner[i, e]
                 else:
                     value = load_rows(side, (0 if e == 0 else 32) + i - 1, 16, 2)
-                store_rows(ext, 8 * i + col, 16, 32, value)
-        full = load_rows(ext, 0, 512, 1).reshape(16, 32, CHANS)
+                store_rows(shift, 8 * i + col, 16, 32, value)
+        full = load_rows(shift, 0, 512, 1).reshape(16, 32, CHANS)
         for b in range(3):
-            rows = full[:, 8 * b : 8 * b + 16, :].reshape(PIXELS, CHANS)
-            taps[3 * b + e, pl.ds(16 * first, PIXELS), :] = rows.astype(jnp.bfloat16)
-    zeros = jnp.zeros((32, CHANS), jnp.bfloat16)
-    for i in range(9):
-        taps[i, pl.ds(0 if first else 256, 32), :] = zeros
+            block = full[:, 8 * b : 8 * b + 16, :].reshape(PIXELS, CHANS)
+            taps[3 * b + e, pl.ds(16 * first, PIXELS), :] = block.astype(jnp.bfloat16)
 
 
 def spread_start(f, r, out, into, width, sems):
@@ -451,7 +482,7 @@
         return out
 
     bufs = take(3)
-    big = [take(13) for _ in range(3)]
+    big = [take(14) for _ in range(3)]
     small = [take(7) for _ in range(3)]
     (full, gbuf, wide, a_taps, g_taps, ext, side, lanes, h_out, h_in, g_out, g_in, before,
      d_out, d_in, l_out, l_in, row1, frame1, row2, frame2, act32, grad32, mask) = take(24)
@@ -492,7 +523,9 @@
     grad_ops = halo_start(f, r, grad32, lanes, g_out, g_in, s_grad)
     waiting += grad_ops
     advance(weights)
+    halo_fill(grad32, ext, g_taps, 0)
     ahead.wait_recv()
+    advance(weights)
     down = act32[...]
     vb = before[...].reshape(PIXELS, CHANS)
     down = down + only(f > 0, dot(vb, wd[:CHANS, :]))
@@ -510,10 +543,9 @@
     total = []
     sums = sum_steps(f, r, sum_rows(mine, mine * mine), total.append, row1, frame1, s_sum1)
     next(sums)
+    next(sums)
     advance(weights)
-    next(sums)
-    halo_finish(f, r, grad_ops, grad32, g_in, ext, side, g_taps, 0)
-    advance(weights)
+    halo_finish(f, r, grad_ops, g_in, ext, side, g_taps, 0)
     for op in down_ops:
         op.wait_recv()
     latent = d_in[...].astype(jnp.float32).reshape(PIXELS, CHANS)
@@ -530,8 +562,10 @@
     wide_act[...] = grown
     act_ops = halo_start(f, r, wide_act, lanes, h_out, h_in, s_act)
     waiting += act_ops
+    halo_fill(wide_act, ext, a_taps, 2)
     advance(weights)
-    halo_finish(f, r, act_ops, wide_act, h_in, ext, side, a_taps, 2)
+    halo_finish(f, r, act_ops, h_in, ext, side, a_taps, 2)
+    advance(weights)
 
     cot = og_ref[...].reshape(PIXELS, CHANS)
     piles = [s[0] for s in big]
@@ -546,6 +580,8 @@
 
         lax.fori_loop(0, high - low, tap, 0)
         pack_rows(gbuf, 2592 * part - CHANS * low, 2, 2 * part, 81, BLOCK, piles)
+        if part == 1:
+            advance(weights)
 
     def scatter(sets, rows, sems, out_ref):
         def run(j, order):
@@ -556,15 +592,14 @@
 
             if rows == 16:
                 return direct_steps(pos, core, order, *s, sems, j * SCATTER_COPIES, out)
-            return scatter_steps(pos, core, order, rows, s[0], s[1], s[2:6], s[6], s[7:11],
-                                 s[11], s[12], sems, j * SCATTER_COPIES, out)
+            return scatter_steps(pos, core, order, rows, s[0], s[1], s[2:6], s[6], s[7], s[8:12],
+                                 s[12], s[13], sems, j * SCATTER_COPIES, out)
 
         return [run(j, order) for j, order in enumerate(ORDERS)]
 
     conv_sum = scatter(big, BLOCK, s_big, gconv_ref)
     advance(conv_sum)
-    for _ in range(3):
-        advance(weights)
+    advance(weights)
 
     def unpack(g, _):
         y_lo, zz = lax.div(g, 4), lax.rem(g, 4)
@@ -597,7 +632,11 @@
         return acc + dot(jnp.concatenate(rows, 1), kernel)
 
     acc = jnp.zeros((PIXELS, CHANS), jnp.float32)
-    acc = lax.fori_loop(0, 9, back, acc)
+    acc = lax.fori_loop(0, 3, back, acc)
+    advance(conv_sum)
+    acc = lax.fori_loop(3, 6, back, acc)
+    advance(conv_sum)
+    acc = lax.fori_loop(6, 9, back, acc)
     xhat = act32[...]
     z = xhat * gain + shift
     sigma = 1.0 / (1.0 + jnp.exp(-z))
@@ -607,12 +646,10 @@
     total2 = []
     sums2 = sum_steps(f, r, sum_rows(pre, pre * xhat), total2.append, row2, frame2, s_sum2)
     next(sums2)
-    advance(conv_sum)
     acc = lax.fori_loop(0, 3, ahead_conv, jnp.zeros((PIXELS, CHANS), jnp.float32))
     next(sums2)
-    acc = lax.fori_loop(3, 9, ahead_conv, acc)
-    code = acc + d_in[...].astype(jnp.float32).reshape(PIXELS, CHANS)
-    code_ref[...] = code.reshape(16, 16, CHANS).astype(jnp.bfloat16)
+    advance(conv_sum)
+    acc = lax.fori_loop(3, 5, ahead_conv, acc)
     next(sums2, None)
     gshift_ref[...] = total2[0][0:1].reshape(CHANS)
     ggain_ref[...] = total2[0][1:2].reshape(CHANS)
@@ -624,6 +661,9 @@
     lat_ops = spread_start(f, r, l_out, l_in, 2, s_lat)
     waiting += lat_ops
     advance(conv_sum)
+    acc = lax.fori_loop(5, 9, ahead_conv, acc)
+    code = acc + d_in[...].astype(jnp.float32).reshape(PIXELS, CHANS)
+    code_ref[...] = code.reshape(16, 16, CHANS).astype(jnp.bfloat16)
     for op in lat_ops:
         op.wait_recv()
     got = l_in[...].astype(jnp.float32)
@@ -640,13 +680,12 @@
     pack_rows(thin, 0, 8, 0, 9, 16, [s[0] for s in small])
     down_sum = scatter(small, 16, s_small, gdown_ref)
     advance(down_sum)
+    advance(conv_sum)
+    advance(down_sum)
     even = dot(lat, wd[CHANS : 2 * CHANS, :], (1, 1))
     odd = dot(lat, wd[2 * CHANS :, :], (1, 1)) + dot(after, wd[:CHANS, :], (1, 1))
     gvideo_ref[0] = even.reshape(2, 128, CHANS).astype(jnp.bfloat16)
     gvideo_ref[1] = odd.reshape(2, 128, CHANS).astype(jnp.bfloat16)
-    advance(down_sum)
-    advance(conv_sum)
-    advance(down_sum)
     advance(down_sum)
     advance(conv_sum)
     interleave(down_sum + conv_sum)
@@ -674,7 +713,7 @@
         pltpu.VMEM((1296, CHANS), f32),
         pltpu.VMEM((9, 288, CHANS), bf16),
         pltpu.VMEM((9, 288, CHANS), bf16),
-        pltpu.VMEM((3, 512, LANES), f32),
+        pltpu.VMEM((9, 512, LANES), f32),
         pltpu.VMEM((3, 64, LANES), f32),
         pltpu.VMEM((3, PIXELS, LANES), f32),
         rows, rows, rows, rows,
@@ -691,7 +730,7 @@
         pltpu.VMEM((PIXELS, CHANS), f32),
         pltpu.VMEM((CHANS, CHANS), f32),
     ]
-    scratch += sems(48) + sems(48) + sems(48) + sems(22) + sems(22) + sems(15) + sems(15)
+    scratch += sems(60) + sems(60) + sems(60) + sems(22) + sems(22) + sems(15) + sems(15)
     scratch += sems(8) + sems(8) + sems(1)
     results = pl.pallas_call(
         section_kernel,

time: 119 us -> 112 us (0.941)
  Pallas kernels: 118 us -> 111 us
    pallas_call x1, Pallas kernels: 116 us -> 109 us  [body(): pl.pallas_call(section_kernel, out_shape=(jax.ShapeDtypeStruct((16, 16, C...]
where the time goes in v4:
time: 112 us
  Pallas kernels  111 us (99%)
    pallas_call x1, Pallas kernels, body(): pl.pallas_call(section_kernel, out_shape=(jax.ShapeDtypeStruct((16, 16, C...  109 us

profile of v4, /device:TPU:0, one launch (start us, length us, event | category | flops | bytes accessed | tf_op | source)
XLA Modules:
  0.0 111.6 jit_solution(15940642803161792355)
XLA Ops:
  0.6 109.0 %shard_map.109 = (bf16[16,16,384]{2,1,0:T(8,128)(2,1)}, bf16[2,2,128,384]{3,2,1,0:T(8,128)(2,1)}, f32[81,384]{1,0:T(8,128)}, f32[9,384]{1,0:T(8,128)}, f32[384]{0:T(512)}, /*index=5*/f32[384]{0:T(512)}) custom-call(bf16[2,2,128,384]{3,2,1,0:T(8,128)(2,1)} %video.1, bf16[1152,384]{1,0:T(8,128)(2,1)} %wd.1, bf16[81,384]{1,0:T(8,128)(2,1)} %w_ref.1, ...), custom_call_target="tpu_custom_call" | custom-call | tf_op jit(solution)/shard_map/pallas_call | solution.py:735
  109.6 2.0 %shard_map.110 = (bf16[16,16,384]{2,1,0:T(8,128)(2,1)}, bf16[2,2,128,384]{3,2,1,0:T(8,128)(2,1)}, f32[81,384]{1,0:T(8,128)}, f32[9,384]{1,0:T(8,128)}, f32[384]{0:T(512)}, /*index=5*/f32[384]{0:T(512)}) custom-call(bf16[16,16,384]{2,1,0:T(8,128)(2,1)} %get-tuple-element.18.refs_0_, bf16[2,2,128,384]{3,2,1,0:T(8,128)(2,1)} %get-tuple-element.19.refs_1_, ...), custom_call_target="tpu_custom_call" | custom-call | tf_op jit(solution)/shard_map/pallas_call | solution.py:752

commit v5 on v4

--- a/solution.py
+++ b/solution.py
@@ -252,10 +252,10 @@
     def f32(*lead):
         return pltpu.VMEM(lead + (rows, LANES), jnp.float32)
 
-    return [bf(2, 4, 4, 4), bf(4, 4, 4), bf(3, 4, 4), f32(4, 4), f32(3, 4), f32(4), f32(3)]
-
-
-def direct_steps(pos, core, order, piles, got, near_p, q, near_q, u, near_u, sems, base, out):
+    return [bf(2, 4, 4, 4), bf(4, 4, 4), bf(3, 4, 4), f32(4, 4), bf(4, 4), bf(3, 4), f32(4), f32(3)]
+
+
+def direct_steps(pos, core, order, piles, got, near_p, q, q_out, near_q, u, near_u, sems, base, out):
     a, b, c = order
     ca = pos[a]
     sent = []
@@ -284,12 +284,13 @@
         op.wait_recv()
         total = total + near_p[n].astype(jnp.float32)
     q[...] = total
-    ops = exchange(b, q, near_q)
+    q_out[...] = total.astype(jnp.bfloat16)
+    ops = exchange(b, q_out, near_q)
     yield
     total = q[pos[b]]
     for n, op in enumerate(ops):
         op.wait_recv()
-        total = total + near_q[n]
+        total = total + near_q[n].astype(jnp.float32)
     u[...] = total
     ops = exchange(c, u, near_u)
     yield
@@ -472,7 +473,7 @@
     lax.fori_loop(0, groups, pack, 0)
 
 
-def section_kernel(video, wd, w_ref, gain_ref, shift_ref, og_ref,
+def section_kernel(video_any, wd_any, w_any, gain_ref, shift_ref, og_any,
                    code_ref, gvideo_ref, gconv_ref, gdown_ref, ggain_ref, gshift_ref, *scratch):
     refs = list(scratch)
 
@@ -483,9 +484,9 @@
 
     bufs = take(3)
     big = [take(14) for _ in range(3)]
-    small = [take(7) for _ in range(3)]
+    small = [take(8) for _ in range(3)]
     (full, gbuf, wide, a_taps, g_taps, ext, side, lanes, h_out, h_in, g_out, g_in, before,
-     d_out, d_in, l_out, l_in, row1, frame1, row2, frame2, act32, grad32, mask) = take(24)
+     d_out, d_in, l_out, l_in, row1, frame1, row2, frame2, act32, grad32, mask, video, wd, w_ref, og_ref, s_local) = take(29)
     sem = [(refs[2 * i], refs[2 * i + 1]) for i in range(len(refs) // 2)]
     s_gather, s_big, s_small, s_sum1, s_sum2, s_down, s_lat, s_act, s_grad, s_video = sem
 
@@ -495,20 +496,28 @@
     peers += [device_at(shifted(pos, "y", s), core) for s in (1, -1)]
     peers += [(lax.rem(f + s, 16), lax.rem(r + t, 8)) for s in (1, 15) for t in (1, 7)]
     arrived = greet(peers)
+    fetch = [pltpu.make_async_copy(src, dst, s_local.at[n]) for n, (src, dst) in enumerate(
+        ((w_any, w_ref), (og_any, og_ref), (video_any, video), (wd_any, wd)))]
+    for op in fetch:
+        op.start()
     waiting = []
 
     def advance(steps):
         for step in steps:
             next(step, None)
 
+    fetch[0].wait()
     for j, (a, b, c) in enumerate(ORDERS):
         block = w_ref[:, LANES * j : LANES * (j + 1)].astype(jnp.float32)
         block = jnp.concatenate([block, jnp.zeros((BLOCK - 81, LANES), jnp.float32)], 0)
         bufs[j][core, pos[a], pos[b], pos[c]] = block.astype(jnp.bfloat16)
+    fetch[1].wait()
     grad32[...] = og_ref[...].astype(jnp.float32).reshape(PIXELS, CHANS)
     group = [jnp.floor((lax.broadcasted_iota(jnp.int32, (CHANS, CHANS), d).astype(jnp.float32) + 0.5)
                        / 12.0) for d in range(2)]
     mask[...] = jnp.where(group[0] == group[1], 1.0, 0.0)
+    fetch[2].wait()
+    fetch[3].wait()
     v0 = video[0].reshape(PIXELS, CHANS)
     v1 = video[1].reshape(PIXELS, CHANS)
     act32[...] = dot(v0, wd[CHANS : 2 * CHANS, :]) + dot(v1, wd[2 * CHANS :, :])
@@ -700,6 +709,7 @@
 
 def body(video, down_weight, conv_weight, norm_gain_vector, norm_shift_vector, output_gradient):
     vmem = pl.BlockSpec(memory_space=pltpu.VMEM)
+    anywhere = pl.BlockSpec(memory_space=pl.ANY)
     bf16, f32 = jnp.bfloat16, jnp.float32
 
     def sems(count):
@@ -729,6 +739,11 @@
         pltpu.VMEM((PIXELS, CHANS), f32),
         pltpu.VMEM((PIXELS, CHANS), f32),
         pltpu.VMEM((CHANS, CHANS), f32),
+        pltpu.VMEM((2, 2, 128, CHANS), bf16),
+        pltpu.VMEM((3 * CHANS, CHANS), bf16),
+        pltpu.VMEM((81, CHANS), bf16),
+        pltpu.VMEM((16, 16, CHANS), bf16),
+        pltpu.SemaphoreType.DMA((4,)),
     ]
     scratch += sems(60) + sems(60) + sems(60) + sems(22) + sems(22) + sems(15) + sems(15)
     scratch += sems(8) + sems(8) + sems(1)
@@ -742,7 +757,7 @@
             jax.ShapeDtypeStruct((CHANS,), f32),
             jax.ShapeDtypeStruct((CHANS,), f32),
         ),
-        in_specs=[vmem] * 6,
+        in_specs=[anywhere] * 3 + [vmem] * 2 + [anywhere],
         out_specs=(vmem,) * 6,
         scratch_shapes=scratch,
         compiler_params=pltpu.CompilerParams(

time: 112 us -> 111 us (level)
  no operation moved by 1% of the time
where the time goes in v5:
time: 111 us
  Pallas kernels  110 us (99%)
    pallas_call x1, Pallas kernels, body(): pl.pallas_call(section_kernel, out_shape=(jax.ShapeDtypeStruct((16, 16, C...  108 us

profile of v5, /device:TPU:0, one launch (start us, length us, event | category | flops | bytes accessed | tf_op | source)
XLA Modules:
  0.0 110.5 jit_solution(17232482166346175872)
XLA Ops:
  0.6 107.8 %shard_map.109 = (bf16[16,16,384]{2,1,0:T(8,128)(2,1)}, bf16[2,2,128,384]{3,2,1,0:T(8,128)(2,1)}, f32[81,384]{1,0:T(8,128)}, f32[9,384]{1,0:T(8,128)}, f32[384]{0:T(512)}, /*index=5*/f32[384]{0:T(512)}) custom-call(bf16[2,2,128,384]{3,2,1,0:T(8,128)(2,1)} %video_any.1, bf16[1152,384]{1,0:T(8,128)(2,1)} %wd_any.1, bf16[81,384]{1,0:T(8,128)(2,1)} %w_any.1, ...), custom_call_target="tpu_custom_call" | custom-call | tf_op jit(solution)/shard_map/pallas_call | solution.py:750
  108.5 2.0 %shard_map.110 = (bf16[16,16,384]{2,1,0:T(8,128)(2,1)}, bf16[2,2,128,384]{3,2,1,0:T(8,128)(2,1)}, f32[81,384]{1,0:T(8,128)}, f32[9,384]{1,0:T(8,128)}, f32[384]{0:T(512)}, /*index=5*/f32[384]{0:T(512)}) custom-call(bf16[16,16,384]{2,1,0:T(8,128)(2,1)} %get-tuple-element.18.refs_0_, bf16[2,2,128,384]{3,2,1,0:T(8,128)(2,1)} %get-tuple-element.19.refs_1_, ...), custom_call_target="tpu_custom_call" | custom-call | tf_op jit(solution)/shard_map/pallas_call | solution.py:767

commit v6 on v5

--- a/solution.py
+++ b/solution.py
@@ -270,15 +270,18 @@
         return [start(ref.at[shifted(pos, axis, s)[axis]], near.at[n],
                       device_at(shifted(pos, axis, s), core)) for n, s in enumerate((1, -1, 2))]
 
-    swap = start(piles.at[1 - core], got, device_at(pos, 1 - core))
-    yield
-    swap.wait_recv()
-    for s in (2, 1, -1):
-        i = shifted(pos, a, s)[a]
+    places = [shifted(pos, a, s)[a] for s in (2, 1, -1, 0)]
+    swaps = [start(piles.at[1 - core, i], got.at[i], device_at(pos, 1 - core)) for i in places]
+    yield
+    ops = []
+    for n, s in enumerate((2, 1, -1)):
+        i = places[n]
+        swaps[n].wait_recv()
         total = piles[core, i].astype(jnp.float32) + got[i].astype(jnp.float32)
         piles[core, i] = total.astype(jnp.bfloat16)
-    ops = exchange(a, piles.at[core], near_p)
-    yield
+        ops.append(start(piles.at[core, i], near_p.at[n], device_at(shifted(pos, a, s), core)))
+    yield
+    swaps[3].wait_recv()
     total = piles[core, ca].astype(jnp.float32) + got[ca].astype(jnp.float32)
     for n, op in enumerate(ops):
         op.wait_recv()

time: 111 us -> 111 us (level)
  no operation moved by 1% of the time
where the time goes in v6:
time: 111 us
  Pallas kernels  110 us (99%)
    pallas_call x1, Pallas kernels, body(): pl.pallas_call(section_kernel, out_shape=(jax.ShapeDtypeStruct((16, 16, C...  108 us

profile of v6, /device:TPU:0, one launch (start us, length us, event | category | flops | bytes accessed | tf_op | source)
XLA Modules:
  0.0 110.6 jit_solution(7533329847666777981)
XLA Ops:
  0.6 107.9 %shard_map.109 = (bf16[16,16,384]{2,1,0:T(8,128)(2,1)}, bf16[2,2,128,384]{3,2,1,0:T(8,128)(2,1)}, f32[81,384]{1,0:T(8,128)}, f32[9,384]{1,0:T(8,128)}, f32[384]{0:T(512)}, /*index=5*/f32[384]{0:T(512)}) custom-call(bf16[2,2,128,384]{3,2,1,0:T(8,128)(2,1)} %video_any.1, bf16[1152,384]{1,0:T(8,128)(2,1)} %wd_any.1, bf16[81,384]{1,0:T(8,128)(2,1)} %w_any.1, ...), custom_call_target="tpu_custom_call" | custom-call | tf_op jit(solution)/shard_map/pallas_call | solution.py:753
  108.6 2.0 %shard_map.110 = (bf16[16,16,384]{2,1,0:T(8,128)(2,1)}, bf16[2,2,128,384]{3,2,1,0:T(8,128)(2,1)}, f32[81,384]{1,0:T(8,128)}, f32[9,384]{1,0:T(8,128)}, f32[384]{0:T(512)}, /*index=5*/f32[384]{0:T(512)}) custom-call(bf16[16,16,384]{2,1,0:T(8,128)(2,1)} %get-tuple-element.18.refs_0_, bf16[2,2,128,384]{3,2,1,0:T(8,128)(2,1)} %get-tuple-element.19.refs_1_, ...), custom_call_target="tpu_custom_call" | custom-call | tf_op jit(solution)/shard_map/pallas_call | solution.py:770
